TPU v7x, 1024 devices: a whole 4x4x32 slice. The times are simulated.
1024 devices in a mesh: gx: 16 (over z_hi, x), gy: 16 (over z_lo, core), gz: 4 (over y).
Axes of the slice: x: 4, y: 4, z: 32 (z_hi: 4, z_lo: 8; z = z_hi * 8 + z_lo), core: 2. Of those that a mesh axis runs over, the one named last changes fastest.
Arguments:
- phase_label: int32 [128, 128, 1024], P('gx', 'gy', 'gz'), may hold values from 0 to 2
- concentration: float32 [128, 128, 1024], P('gx', 'gy', 'gz'), may hold values from 0.3 to 3
- phase_factor: float32 [3], replicated, may hold values from 0.05 to 1
- potential: float32 [3, 128, 128, 1024], P(None, 'gx', 'gy', 'gz'), may hold values from -6 to 6
- source: float32 [3, 128, 128, 1024], P(None, 'gx', 'gy', 'gz'), may hold values from -6 to 6
Outputs:
- level_correction: float32 [3, 64, 64, 512], P(None, 'gx', 'gy', 'gz')
- coarse_correction: float32 [3, 16, 16, 128], P(None, 'gx', 'gy')
All inputs are finite; a program needn't handle non-finite values.
Results may differ from a plain program's by a relative error of at most 0.00002.
Values sent between devices are 32-bit elements; how exact they have to be, the bound alone decides.
A program may use at most 32 MiB of HBM per device.

v0:
```python
import jax
import jax.numpy as jnp
from jax import lax
from jax.sharding import PartitionSpec as P

SWEEPS = 4


mass_term = 0.05
damping = 0.7
decay_rate = 0.3


def with_halo(cells, sides, width):
    for axis, dim in sides:
        count = lax.axis_size(axis)
        ends = count - 1
        head = lax.slice_in_dim(cells, 0, width, axis=dim)
        tail = lax.slice_in_dim(cells, cells.shape[dim] - width, cells.shape[dim], axis=dim)
        cells = jnp.concatenate(
            [
                lax.ppermute(tail, axis, [(i, (i + 1) % count) for i in range(ends)]),
                cells,
                lax.ppermute(head, axis, [((i + 1) % count, i) for i in range(ends)]),
            ],
            axis=dim,
        )
    return cells


def stencil_from_padded(padded):
    center = padded[1:-1, 1:-1, 1:-1]

    def harmonic(other):
        return 2.0 * center * other / (center + other)

    parts = [
        jnp.full(center.shape, mass_term, jnp.float32),
        harmonic(padded[:-2, 1:-1, 1:-1]),
        harmonic(padded[2:, 1:-1, 1:-1]),
        harmonic(padded[1:-1, :-2, 1:-1]),
        harmonic(padded[1:-1, 2:, 1:-1]),
        harmonic(padded[1:-1, 1:-1, :-2]),
        harmonic(padded[1:-1, 1:-1, 2:]),
    ]
    return jnp.stack(parts)


def apply_padded(stencil, values, padded):
    total = stencil[0] * values
    total = total + stencil[1] * (values - padded[:, :-2, 1:-1, 1:-1])
    total = total + stencil[2] * (values - padded[:, 2:, 1:-1, 1:-1])
    total = total + stencil[3] * (values - padded[:, 1:-1, :-2, 1:-1])
    total = total + stencil[4] * (values - padded[:, 1:-1, 2:, 1:-1])
    total = total + stencil[5] * (values - padded[:, 1:-1, 1:-1, :-2])
    total = total + stencil[6] * (values - padded[:, 1:-1, 1:-1, 2:])
    return total


def every_other(values, which, axis):
    return lax.slice_in_dim(values, which, values.shape[axis], 2, axis)


def pair_sum(values, axes):
    for axis in axes:
        values = every_other(values, 0, axis) + every_other(values, 1, axis)
    return values


def restrict(values):
    return pair_sum(values, (1, 2, 3))


def galerkin(stencil):
    parts = [
        pair_sum(stencil[0], (0, 1, 2)),
        pair_sum(every_other(stencil[1], 0, 0), (1, 2)),
        pair_sum(every_other(stencil[2], 1, 0), (1, 2)),
        pair_sum(every_other(stencil[3], 0, 1), (0, 2)),
        pair_sum(every_other(stencil[4], 1, 1), (0, 2)),
        pair_sum(every_other(stencil[5], 0, 2), (0, 1)),
        pair_sum(every_other(stencil[6], 1, 2), (0, 1)),
    ]
    return jnp.stack(parts)


def level_pad(values):
    return with_halo(values, (("gx", 1), ("gy", 2), ("gz", 3)), 1)


def split_pad(values):
    return with_halo(values, (("gx", 1), ("gy", 2), ("gz", 3)), 1)


def smooth(residual, stencil):
    diagonal = jnp.sum(stencil, axis=0)
    correction = damping * residual / diagonal
    correction = (
        correction
        + damping * (residual - apply_padded(stencil, correction, level_pad(correction))) / diagonal
    )
    return (correction, residual - apply_padded(stencil, correction, level_pad(correction)))


def jacobi(residual, stencil, padder):
    diagonal = jnp.sum(stencil, axis=0)
    correction = damping * residual / diagonal
    for sweep in range(SWEEPS - 1):
        correction = (
            correction
            + damping
            * (residual - apply_padded(stencil, correction, padder(correction)))
            / diagonal
        )
    return correction


def local(phase_label, concentration, phase_factor, potential, source):
    lookup = jnp.zeros(phase_label.shape, jnp.float32)
    for index in range(3):
        lookup = lookup + jnp.where(phase_label == index, phase_factor[index], 0.0)
    conduct = lookup * concentration * jnp.exp(-decay_rate * concentration)
    conduct_pad = with_halo(conduct, (("gx", 0), ("gy", 1), ("gz", 2)), 1)
    potential_pad = with_halo(potential, (("gx", 1), ("gy", 2), ("gz", 3)), 1)
    stencil0 = stencil_from_padded(conduct_pad)
    first = restrict(source - apply_padded(stencil0, potential, potential_pad))
    stencil1 = galerkin(stencil0)
    level_correction, left1 = smooth(first, stencil1)
    stencil2 = galerkin(stencil1)
    second, left2 = smooth(restrict(left1), stencil2)
    stencil3 = galerkin(stencil2)
    third = restrict(left2)
    own_part = jacobi(third, stencil3, split_pad)
    coarse_correction = lax.all_gather(own_part, "gz", axis=3, tiled=True)
    return (level_correction, coarse_correction)


def solution(mesh):
    placed = (
        P("gx", "gy", "gz"),
        P("gx", "gy", "gz"),
        P(),
        P(None, "gx", "gy", "gz"),
        P(None, "gx", "gy", "gz"),
    )
    return jax.shard_map(
        local,
        mesh=mesh,
        in_specs=placed,
        out_specs=(P(None, "gx", "gy", "gz"), P(None, "gx", "gy", None)),
        check_vma=False,
    )
```

profile of v0, /device:TPU:134, one launch (start us, length us, event | category | flops | bytes accessed | tf_op | source)
XLA Modules:
  0.0 356.0 jit_solution(2599451861370506754)
XLA Ops:
  4.9 15.6 %collective-permute-start = (f32[1,8,256]{2,1,0:T(8,128)S(1)}, f32[1,8,256]{2,1,0:T(8,128)S(1)}, u32[]{:S(2)}, u32[]{:S(2)}) collective-permute-start(f32[1,8,256]{2,1,0:T(8,128)S(1)} %get-tuple-element.62), channel_id=1, source_target_pairs={{0,64},{64,128},{128,192},{192,256},{256,320},{320,384},{384,448},... | collective-permute-start | bytes 24584 | tf_op jit(solution)/shard_map/ppermute | solution.py:22
  22.5 14.5 %collective-permute-done.2 = f32[1,8,256]{2,1,0:T(8,128)S(1)} collective-permute-done((f32[1,8,256]{2,1,0:T(8,128)S(1)}, f32[1,8,256]{2,1,0:T(8,128)S(1)}, u32[]{:S(2)}, u32[]{:S(2)}) %collective-permute-start.2) | collective-permute-done | bytes 8224 | tf_op jit(solution)/shard_map/ppermute | solution.py:24
  38.9 4.9 %collective-permute-start.6 = (f32[10,1,256]{2,1,0:T(1,128)S(1)}, f32[10,1,256]{2,1,0:T(1,128)S(1)}, u32[]{:S(2)}, u32[]{:S(2)}) collective-permute-start(f32[10,1,256]{2,1,0:T(1,128)S(1)} %get-tuple-element.52), channel_id=1, source_target_pairs={{4,0},{8,4},{12,8},{16,12},{20,16},{24,20},{28,24},{32,28},{36,32}... | collective-permute-start | bytes 30728 | tf_op jit(solution)/shard_map/ppermute | solution.py:24
  45.7 3.9 %collective-permute-start.3 = (f32[3,1,8,256]{3,2,1,0:T(8,128)S(1)}, f32[3,1,8,256]{3,2,1,0:T(8,128)S(1)}, u32[]{:S(2)}, u32[]{:S(2)}) collective-permute-start(f32[3,1,8,256]{3,2,1,0:T(8,128)S(1)} %get-tuple-element.45), channel_id=1, source_target_pairs={{64,0},{128,64},{192,128},{256,192},{320,256},{384,320},{448,384},... | collective-permute-start | bytes 73736 | tf_op jit(solution)/shard_map/ppermute | solution.py:24
  51.1 4.6 %collective-permute-start.8 = (f32[10,10,1]{2,1,0:T(8,128)S(1)}, f32[10,10,1]{2,1,0:T(8,128)S(1)}, u32[]{:S(2)}, u32[]{:S(2)}) collective-permute-start(f32[10,10,1]{2,1,0:T(8,128)S(1)} %get-tuple-element.48), channel_id=1, source_target_pairs={{0,1},{1,2},{2,3},{4,5},{5,6},{6,7},{8,9},{9,10},{10,11},{12,13},{... | collective-permute-start | bytes 1208 | tf_op jit(solution)/shard_map/ppermute | solution.py:22
  66.1 4.8 %collective-permute-start.7 = (f32[3,10,1,256]{3,2,1,0:T(1,128)S(1)}, f32[3,10,1,256]{3,2,1,0:T(1,128)S(1)}, u32[]{:S(2)}, u32[]{:S(2)}) collective-permute-start(f32[3,10,1,256]{3,2,1,0:T(1,128)S(1)} %get-tuple-element.44), channel_id=1, source_target_pairs={{4,0},{8,4},{12,8},{16,12},{20,16},{24,20},{28,24},{32,28},{36,32}... | collective-permute-start | bytes 92168 | tf_op jit(solution)/shard_map/ppermute | solution.py:24
  74.0 4.6 %collective-permute-start.9 = (f32[3,10,10,1]{3,0,2,1:T(4,128)S(1)}, f32[3,10,10,1]{3,0,2,1:T(4,128)S(1)}, u32[]{:S(2)}, u32[]{:S(2)}) collective-permute-start(f32[3,10,10,1]{3,0,2,1:T(4,128)S(1)} %get-tuple-element.41), channel_id=1, source_target_pairs={{0,1},{1,2},{2,3},{4,5},{5,6},{6,7},{8,9},{9,10},{10,11},{12,13},{... | collective-permute-start | bytes 3608 | tf_op jit(solution)/shard_map/ppermute | solution.py:22
  85.3 11.3 %collective-permute-start.12 = (f32[3,1,4,128]{3,2,1,0:T(4,128)S(1)}, f32[3,1,4,128]{3,2,1,0:T(4,128)S(1)}, u32[]{:S(2)}, u32[]{:S(2)}) collective-permute-start(f32[3,1,4,128]{3,2,1,0:T(4,128)S(1)} %get-tuple-element.73), channel_id=1, source_target_pairs={{0,64},{64,128},{128,192},{192,256},{256,320},{320,384},{384,448},... | collective-permute-start | bytes 18440 | tf_op jit(solution)/shard_map/ppermute | solution.py:22
  98.8 14.2 %collective-permute-done.13 = f32[3,1,4,128]{3,2,1,0:T(4,128)S(1)} collective-permute-done((f32[3,1,4,128]{3,2,1,0:T(4,128)S(1)}, f32[3,1,4,128]{3,2,1,0:T(4,128)S(1)}, u32[]{:S(2)}, u32[]{:S(2)}) %collective-permute-start.13) | collective-permute-done | bytes 6176 | tf_op jit(solution)/shard_map/ppermute | solution.py:24
  114.9 4.9 %collective-permute-start.15 = (f32[3,6,1,128]{3,2,1,0:T(1,128)S(1)}, f32[3,6,1,128]{3,2,1,0:T(1,128)S(1)}, u32[]{:S(2)}, u32[]{:S(2)}) collective-permute-start(f32[3,6,1,128]{3,2,1,0:T(1,128)S(1)} %get-tuple-element.66), channel_id=1, source_target_pairs={{4,0},{8,4},{12,8},{16,12},{20,16},{24,20},{28,24},{32,28},{36,32}... | collective-permute-start | bytes 27656 | tf_op jit(solution)/shard_map/ppermute | solution.py:24
  121.3 4.4 %collective-permute-start.16 = (f32[3,6,6,1]{3,2,1,0:T(8,128)S(1)}, f32[3,6,6,1]{3,2,1,0:T(8,128)S(1)}, u32[]{:S(2)}, u32[]{:S(2)}) collective-permute-start(f32[3,6,6,1]{3,2,1,0:T(8,128)S(1)} %get-tuple-element.56), channel_id=1, source_target_pairs={{0,1},{1,2},{2,3},{4,5},{5,6},{6,7},{8,9},{9,10},{10,11},{12,13},{... | collective-permute-start | bytes 1304 | tf_op jit(solution)/shard_map/ppermute | solution.py:22
  127.6 4.3 %collective-permute-done.17 = f32[3,6,6,1]{3,2,1,0:T(8,128)S(1)} collective-permute-done((f32[3,6,6,1]{3,2,1,0:T(8,128)S(1)}, f32[3,6,6,1]{3,2,1,0:T(8,128)S(1)}, u32[]{:S(2)}, u32[]{:S(2)}) %collective-permute-start.17) | collective-permute-done | bytes 464 | tf_op jit(solution)/shard_map/ppermute | solution.py:24
  138.0 12.5 %collective-permute-done.19 = f32[3,1,4,128]{3,2,1,0:T(4,128)S(1)} collective-permute-done((f32[3,1,4,128]{3,2,1,0:T(4,128)S(1)}, f32[3,1,4,128]{3,2,1,0:T(4,128)S(1)}, u32[]{:S(2)}, u32[]{:S(2)}) %collective-permute-start.19) | collective-permute-done | bytes 6176 | tf_op jit(solution)/shard_map/ppermute | solution.py:24
  152.4 4.9 %collective-permute-start.21 = (f32[3,6,1,128]{3,2,1,0:T(1,128)S(1)}, f32[3,6,1,128]{3,2,1,0:T(1,128)S(1)}, u32[]{:S(2)}, u32[]{:S(2)}) collective-permute-start(f32[3,6,1,128]{3,2,1,0:T(1,128)S(1)} %get-tuple-element.64), channel_id=1, source_target_pairs={{4,0},{8,4},{12,8},{16,12},{20,16},{24,20},{28,24},{32,28},{36,32}... | collective-permute-start | bytes 27656 | tf_op jit(solution)/shard_map/ppermute | solution.py:24
  164.5 4.3 %collective-permute-done.23 = f32[3,6,6,1]{3,2,1,0:T(8,128)S(1)} collective-permute-done((f32[3,6,6,1]{3,2,1,0:T(8,128)S(1)}, f32[3,6,6,1]{3,2,1,0:T(8,128)S(1)}, u32[]{:S(2)}, u32[]{:S(2)}) %collective-permute-start.23) | collective-permute-done | bytes 464 | tf_op jit(solution)/shard_map/ppermute | solution.py:24
  176.1 12.4 %collective-permute-done.25 = f32[3,1,2,64]{3,2,1,0:T(2,128)S(1)} collective-permute-done((f32[3,1,2,64]{3,2,1,0:T(2,128)S(1)}, f32[3,1,2,64]{3,2,1,0:T(2,128)S(1)}, u32[]{:S(2)}, u32[]{:S(2)}) %collective-permute-start.25) | collective-permute-done | bytes 1568 | tf_op jit(solution)/shard_map/ppermute | solution.py:24
  190.4 4.9 %collective-permute-start.27 = (f32[3,4,1,64]{3,2,1,0:T(1,128)S(1)}, f32[3,4,1,64]{3,2,1,0:T(1,128)S(1)}, u32[]{:S(2)}, u32[]{:S(2)}) collective-permute-start(f32[3,4,1,64]{3,2,1,0:T(1,128)S(1)} %get-tuple-element.84), channel_id=1, source_target_pairs={{4,0},{8,4},{12,8},{16,12},{20,16},{24,20},{28,24},{32,28},{36,32}... | collective-permute-start | bytes 9224 | tf_op jit(solution)/shard_map/ppermute | solution.py:24
  201.7 4.2 %collective-permute-done.29 = f32[3,4,4,1]{3,2,1,0:T(4,128)S(1)} collective-permute-done((f32[3,4,4,1]{3,2,1,0:T(4,128)S(1)}, f32[3,4,4,1]{3,2,1,0:T(4,128)S(1)}, u32[]{:S(2)}, u32[]{:S(2)}) %collective-permute-start.29) | collective-permute-done | bytes 224 | tf_op jit(solution)/shard_map/ppermute | solution.py:24
  211.9 12.4 %collective-permute-done.31 = f32[3,1,2,64]{3,2,1,0:T(2,128)S(1)} collective-permute-done((f32[3,1,2,64]{3,2,1,0:T(2,128)S(1)}, f32[3,1,2,64]{3,2,1,0:T(2,128)S(1)}, u32[]{:S(2)}, u32[]{:S(2)}) %collective-permute-start.31) | collective-permute-done | bytes 1568 | tf_op jit(solution)/shard_map/ppermute | solution.py:24
  226.2 4.9 %collective-permute-start.33 = (f32[3,4,1,64]{3,2,1,0:T(1,128)S(1)}, f32[3,4,1,64]{3,2,1,0:T(1,128)S(1)}, u32[]{:S(2)}, u32[]{:S(2)}) collective-permute-start(f32[3,4,1,64]{3,2,1,0:T(1,128)S(1)} %get-tuple-element.82), channel_id=1, source_target_pairs={{4,0},{8,4},{12,8},{16,12},{20,16},{24,20},{28,24},{32,28},{36,32}... | collective-permute-start | bytes 9224 | tf_op jit(solution)/shard_map/ppermute | solution.py:24
  235.9 4.2 %collective-permute-done.35 = f32[3,4,4,1]{3,2,1,0:T(4,128)S(1)} collective-permute-done((f32[3,4,4,1]{3,2,1,0:T(4,128)S(1)}, f32[3,4,4,1]{3,2,1,0:T(4,128)S(1)}, u32[]{:S(2)}, u32[]{:S(2)}) %collective-permute-start.35) | collective-permute-done | bytes 224 | tf_op jit(solution)/shard_map/ppermute | solution.py:24
  243.0 3.9 %collective-permute-start.37 = (f32[3,1,1,32]{3,2,1,0:T(1,128)S(1)}, f32[3,1,1,32]{3,2,1,0:T(1,128)S(1)}, u32[]{:S(2)}, u32[]{:S(2)}) collective-permute-start(f32[3,1,1,32]{3,2,1,0:T(1,128)S(1)} %get-tuple-element.12), channel_id=1, source_target_pairs={{64,0},{128,64},{192,128},{256,192},{320,256},{384,320},{448,384},... | collective-permute-start | bytes 1160 | tf_op jit(solution)/shard_map/ppermute | solution.py:24
  247.0 12.4 %collective-permute-done.37 = f32[3,1,1,32]{3,2,1,0:T(1,128)S(1)} collective-permute-done((f32[3,1,1,32]{3,2,1,0:T(1,128)S(1)}, f32[3,1,1,32]{3,2,1,0:T(1,128)S(1)}, u32[]{:S(2)}, u32[]{:S(2)}) %collective-permute-start.37) | collective-permute-done | bytes 416 | tf_op jit(solution)/shard_map/ppermute | solution.py:24
  261.3 4.9 %collective-permute-start.39 = (f32[3,3,1,32]{3,2,1,0:T(1,128)S(1)}, f32[3,3,1,32]{3,2,1,0:T(1,128)S(1)}, u32[]{:S(2)}, u32[]{:S(2)}) collective-permute-start(f32[3,3,1,32]{3,2,1,0:T(1,128)S(1)} %pad_maximum_fusion.115), channel_id=1, source_target_pairs={{4,0},{8,4},{12,8},{16,12},{20,16},{24,20},{28,24},{32,28},{36,32}... | collective-permute-start | bytes 3464 | tf_op jit(solution)/shard_map/ppermute | solution.py:24
  270.9 4.2 %collective-permute-done.41 = f32[3,3,3,1]{3,2,1,0:T(4,128)S(1)} collective-permute-done((f32[3,3,3,1]{3,2,1,0:T(4,128)S(1)}, f32[3,3,3,1]{3,2,1,0:T(4,128)S(1)}, u32[]{:S(2)}, u32[]{:S(2)}) %collective-permute-start.41) | collective-permute-done | bytes 140 | tf_op jit(solution)/shard_map/ppermute | solution.py:24
  281.1 12.4 %collective-permute-done.43 = f32[3,1,1,32]{3,2,1,0:T(1,128)S(1)} collective-permute-done((f32[3,1,1,32]{3,2,1,0:T(1,128)S(1)}, f32[3,1,1,32]{3,2,1,0:T(1,128)S(1)}, u32[]{:S(2)}, u32[]{:S(2)}) %collective-permute-start.43) | collective-permute-done | bytes 416 | tf_op jit(solution)/shard_map/ppermute | solution.py:24
  295.4 4.9 %collective-permute-start.45 = (f32[3,3,1,32]{3,2,1,0:T(1,128)S(1)}, f32[3,3,1,32]{3,2,1,0:T(1,128)S(1)}, u32[]{:S(2)}, u32[]{:S(2)}) collective-permute-start(f32[3,3,1,32]{3,2,1,0:T(1,128)S(1)} %pad_maximum_fusion.116), channel_id=1, source_target_pairs={{4,0},{8,4},{12,8},{16,12},{20,16},{24,20},{28,24},{32,28},{36,32}... | collective-permute-start | bytes 3464 | tf_op jit(solution)/shard_map/ppermute | solution.py:24
  305.0 4.2 %collective-permute-done.47 = f32[3,3,3,1]{3,2,1,0:T(4,128)S(1)} collective-permute-done((f32[3,3,3,1]{3,2,1,0:T(4,128)S(1)}, f32[3,3,3,1]{3,2,1,0:T(4,128)S(1)}, u32[]{:S(2)}, u32[]{:S(2)}) %collective-permute-start.47) | collective-permute-done | bytes 140 | tf_op jit(solution)/shard_map/ppermute | solution.py:24
  315.2 12.4 %collective-permute-done.49 = f32[3,1,1,32]{3,2,1,0:T(1,128)S(1)} collective-permute-done((f32[3,1,1,32]{3,2,1,0:T(1,128)S(1)}, f32[3,1,1,32]{3,2,1,0:T(1,128)S(1)}, u32[]{:S(2)}, u32[]{:S(2)}) %collective-permute-start.49) | collective-permute-done | bytes 416 | tf_op jit(solution)/shard_map/ppermute | solution.py:24
  329.5 4.9 %collective-permute-start.51 = (f32[3,3,1,32]{3,2,1,0:T(1,128)S(1)}, f32[3,3,1,32]{3,2,1,0:T(1,128)S(1)}, u32[]{:S(2)}, u32[]{:S(2)}) collective-permute-start(f32[3,3,1,32]{3,2,1,0:T(1,128)S(1)} %pad_maximum_fusion.117), channel_id=1, source_target_pairs={{4,0},{8,4},{12,8},{16,12},{20,16},{24,20},{28,24},{32,28},{36,32}... | collective-permute-start | bytes 3464 | tf_op jit(solution)/shard_map/ppermute | solution.py:24
  339.1 4.2 %collective-permute-done.53 = f32[3,3,3,1]{3,2,1,0:T(4,128)S(1)} collective-permute-done((f32[3,3,3,1]{3,2,1,0:T(4,128)S(1)}, f32[3,3,3,1]{3,2,1,0:T(4,128)S(1)}, u32[]{:S(2)}, u32[]{:S(2)}) %collective-permute-start.53) | collective-permute-done | bytes 140 | tf_op jit(solution)/shard_map/ppermute | solution.py:24
  343.5 11.9 %all_gather.3 = f32[3,1,1,128]{0,2,1,3:T(1,128)S(1)} all-gather(f32[3,1,1,32]{0,2,1,3:T(1,128)S(1)} %copy.408), channel_id=1, replica_groups=mesh['gx'=16,'gy'=16,'gz'=4] {'gz'}, dimensions={3}, use_global_device_ids=true | all-gather | bytes 1920 | tf_op jit(solution)/shard_map/all_gather | solution.py:134
  (229 shorter events, 117.9 us)
Async XLA Ops:
  4.9 17.6 %collective-permute-start = (f32[1,8,256]{2,1,0:T(8,128)S(1)}, f32[1,8,256]{2,1,0:T(8,128)S(1)}, u32[]{:S(2)}, u32[]{:S(2)}) collective-permute-start(f32[1,8,256]{2,1,0:T(8,128)S(1)} %get-tuple-element.62), channel_id=1, source_target_pairs={{0,64},{64,128},{128,192},{192,256},{256,320},{320,384},{384,448},... | collective-permute-start | bytes 24584 | tf_op jit(solution)/shard_map/ppermute | solution.py:22
  20.5 16.4 %collective-permute-start.2 = (f32[1,8,256]{2,1,0:T(8,128)S(1)}, f32[1,8,256]{2,1,0:T(8,128)S(1)}, u32[]{:S(2)}, u32[]{:S(2)}) collective-permute-start(f32[1,8,256]{2,1,0:T(8,128)S(1)} %get-tuple-element.61), channel_id=1, source_target_pairs={{64,0},{128,64},{192,128},{256,192},{320,256},{384,320},{448,384},... | collective-permute-start | bytes 24584 | tf_op jit(solution)/shard_map/ppermute | solution.py:24
  36.9 12.7 %collective-permute-start.4 = (f32[10,1,256]{2,1,0:T(1,128)S(1)}, f32[10,1,256]{2,1,0:T(1,128)S(1)}, u32[]{:S(2)}, u32[]{:S(2)}) collective-permute-start(f32[10,1,256]{2,1,0:T(1,128)S(1)} %get-tuple-element.53), channel_id=1, source_target_pairs={{0,4},{4,8},{8,12},{12,16},{16,20},{20,24},{24,28},{28,32},{32,36}... | collective-permute-start | bytes 30728 | tf_op jit(solution)/shard_map/ppermute | solution.py:22
  38.9 10.8 %collective-permute-start.6 = (f32[10,1,256]{2,1,0:T(1,128)S(1)}, f32[10,1,256]{2,1,0:T(1,128)S(1)}, u32[]{:S(2)}, u32[]{:S(2)}) collective-permute-start(f32[10,1,256]{2,1,0:T(1,128)S(1)} %get-tuple-element.52), channel_id=1, source_target_pairs={{4,0},{8,4},{12,8},{16,12},{20,16},{24,20},{28,24},{32,28},{36,32}... | collective-permute-start | bytes 30728 | tf_op jit(solution)/shard_map/ppermute | solution.py:24
  43.8 16.4 %collective-permute-start.1 = (f32[3,1,8,256]{3,2,1,0:T(8,128)S(1)}, f32[3,1,8,256]{3,2,1,0:T(8,128)S(1)}, u32[]{:S(2)}, u32[]{:S(2)}) collective-permute-start(f32[3,1,8,256]{3,2,1,0:T(8,128)S(1)} %get-tuple-element.46), channel_id=1, source_target_pairs={{0,64},{64,128},{128,192},{192,256},{256,320},{320,384},{384,448},... | collective-permute-start | bytes 73736 | tf_op jit(solution)/shard_map/ppermute | solution.py:22
  45.7 16.8 %collective-permute-start.3 = (f32[3,1,8,256]{3,2,1,0:T(8,128)S(1)}, f32[3,1,8,256]{3,2,1,0:T(8,128)S(1)}, u32[]{:S(2)}, u32[]{:S(2)}) collective-permute-start(f32[3,1,8,256]{3,2,1,0:T(8,128)S(1)} %get-tuple-element.45), channel_id=1, source_target_pairs={{64,0},{128,64},{192,128},{256,192},{320,256},{384,320},{448,384},... | collective-permute-start | bytes 73736 | tf_op jit(solution)/shard_map/ppermute | solution.py:24
  49.8 7.5 %collective-permute-start.10 = (f32[10,10,1]{2,1,0:T(8,128)S(1)}, f32[10,10,1]{2,1,0:T(8,128)S(1)}, u32[]{:S(2)}, u32[]{:S(2)}) collective-permute-start(f32[10,10,1]{2,1,0:T(8,128)S(1)} %get-tuple-element.47), channel_id=1, source_target_pairs={{1,0},{2,1},{3,2},{5,4},{6,5},{7,6},{9,8},{10,9},{11,10},{13,12},{... | collective-permute-start | bytes 1208 | tf_op jit(solution)/shard_map/ppermute | solution.py:24
  51.1 6.6 %collective-permute-start.8 = (f32[10,10,1]{2,1,0:T(8,128)S(1)}, f32[10,10,1]{2,1,0:T(8,128)S(1)}, u32[]{:S(2)}, u32[]{:S(2)}) collective-permute-start(f32[10,10,1]{2,1,0:T(8,128)S(1)} %get-tuple-element.48), channel_id=1, source_target_pairs={{0,1},{1,2},{2,3},{4,5},{5,6},{6,7},{8,9},{9,10},{10,11},{12,13},{... | collective-permute-start | bytes 1208 | tf_op jit(solution)/shard_map/ppermute | solution.py:22
  62.5 8.4 %collective-permute-start.5 = (f32[3,10,1,256]{3,2,1,0:T(1,128)S(1)}, f32[3,10,1,256]{3,2,1,0:T(1,128)S(1)}, u32[]{:S(2)}, u32[]{:S(2)}) collective-permute-start(f32[3,10,1,256]{3,2,1,0:T(1,128)S(1)} %get-tuple-element.43), channel_id=1, source_target_pairs={{0,4},{4,8},{8,12},{12,16},{16,20},{20,24},{24,28},{28,32},{32,36}... | collective-permute-start | bytes 92168 | tf_op jit(solution)/shard_map/ppermute | solution.py:22
  66.1 6.4 %collective-permute-start.7 = (f32[3,10,1,256]{3,2,1,0:T(1,128)S(1)}, f32[3,10,1,256]{3,2,1,0:T(1,128)S(1)}, u32[]{:S(2)}, u32[]{:S(2)}) collective-permute-start(f32[3,10,1,256]{3,2,1,0:T(1,128)S(1)} %get-tuple-element.44), channel_id=1, source_target_pairs={{4,0},{8,4},{12,8},{16,12},{20,16},{24,20},{28,24},{32,28},{36,32}... | collective-permute-start | bytes 92168 | tf_op jit(solution)/shard_map/ppermute | solution.py:24
  72.7 8.3 %collective-permute-start.11 = (f32[3,10,10,1]{3,0,2,1:T(4,128)S(1)}, f32[3,10,10,1]{3,0,2,1:T(4,128)S(1)}, u32[]{:S(2)}, u32[]{:S(2)}) collective-permute-start(f32[3,10,10,1]{3,0,2,1:T(4,128)S(1)} %get-tuple-element.42), channel_id=1, source_target_pairs={{1,0},{2,1},{3,2},{5,4},{6,5},{7,6},{9,8},{10,9},{11,10},{13,12},{... | collective-permute-start | bytes 3608 | tf_op jit(solution)/shard_map/ppermute | solution.py:24
  74.0 8.2 %collective-permute-start.9 = (f32[3,10,10,1]{3,0,2,1:T(4,128)S(1)}, f32[3,10,10,1]{3,0,2,1:T(4,128)S(1)}, u32[]{:S(2)}, u32[]{:S(2)}) collective-permute-start(f32[3,10,10,1]{3,0,2,1:T(4,128)S(1)} %get-tuple-element.41), channel_id=1, source_target_pairs={{0,1},{1,2},{2,3},{4,5},{5,6},{6,7},{8,9},{9,10},{10,11},{12,13},{... | collective-permute-start | bytes 3608 | tf_op jit(solution)/shard_map/ppermute | solution.py:22
  85.3 13.4 %collective-permute-start.12 = (f32[3,1,4,128]{3,2,1,0:T(4,128)S(1)}, f32[3,1,4,128]{3,2,1,0:T(4,128)S(1)}, u32[]{:S(2)}, u32[]{:S(2)}) collective-permute-start(f32[3,1,4,128]{3,2,1,0:T(4,128)S(1)} %get-tuple-element.73), channel_id=1, source_target_pairs={{0,64},{64,128},{128,192},{192,256},{256,320},{320,384},{384,448},... | collective-permute-start | bytes 18440 | tf_op jit(solution)/shard_map/ppermute | solution.py:22
  96.6 16.3 %collective-permute-start.13 = (f32[3,1,4,128]{3,2,1,0:T(4,128)S(1)}, f32[3,1,4,128]{3,2,1,0:T(4,128)S(1)}, u32[]{:S(2)}, u32[]{:S(2)}) collective-permute-start(f32[3,1,4,128]{3,2,1,0:T(4,128)S(1)} %get-tuple-element.74), channel_id=1, source_target_pairs={{64,0},{128,64},{192,128},{256,192},{320,256},{384,320},{448,384},... | collective-permute-start | bytes 18440 | tf_op jit(solution)/shard_map/ppermute | solution.py:24
  113.0 7.0 %collective-permute-start.14 = (f32[3,6,1,128]{3,2,1,0:T(1,128)S(1)}, f32[3,6,1,128]{3,2,1,0:T(1,128)S(1)}, u32[]{:S(2)}, u32[]{:S(2)}) collective-permute-start(f32[3,6,1,128]{3,2,1,0:T(1,128)S(1)} %get-tuple-element.65), channel_id=1, source_target_pairs={{0,4},{4,8},{8,12},{12,16},{16,20},{20,24},{24,28},{28,32},{32,36}... | collective-permute-start | bytes 27656 | tf_op jit(solution)/shard_map/ppermute | solution.py:22
  114.9 6.2 %collective-permute-start.15 = (f32[3,6,1,128]{3,2,1,0:T(1,128)S(1)}, f32[3,6,1,128]{3,2,1,0:T(1,128)S(1)}, u32[]{:S(2)}, u32[]{:S(2)}) collective-permute-start(f32[3,6,1,128]{3,2,1,0:T(1,128)S(1)} %get-tuple-element.66), channel_id=1, source_target_pairs={{4,0},{8,4},{12,8},{16,12},{20,16},{24,20},{28,24},{32,28},{36,32}... | collective-permute-start | bytes 27656 | tf_op jit(solution)/shard_map/ppermute | solution.py:24
  121.3 6.4 %collective-permute-start.16 = (f32[3,6,6,1]{3,2,1,0:T(8,128)S(1)}, f32[3,6,6,1]{3,2,1,0:T(8,128)S(1)}, u32[]{:S(2)}, u32[]{:S(2)}) collective-permute-start(f32[3,6,6,1]{3,2,1,0:T(8,128)S(1)} %get-tuple-element.56), channel_id=1, source_target_pairs={{0,1},{1,2},{2,3},{4,5},{5,6},{6,7},{8,9},{9,10},{10,11},{12,13},{... | collective-permute-start | bytes 1304 | tf_op jit(solution)/shard_map/ppermute | solution.py:22
  125.7 6.2 %collective-permute-start.17 = (f32[3,6,6,1]{3,2,1,0:T(8,128)S(1)}, f32[3,6,6,1]{3,2,1,0:T(8,128)S(1)}, u32[]{:S(2)}, u32[]{:S(2)}) collective-permute-start(f32[3,6,6,1]{3,2,1,0:T(8,128)S(1)} %get-tuple-element.57), channel_id=1, source_target_pairs={{1,0},{2,1},{3,2},{5,4},{6,5},{7,6},{9,8},{10,9},{11,10},{13,12},{... | collective-permute-start | bytes 1304 | tf_op jit(solution)/shard_map/ppermute | solution.py:24
  134.0 16.4 %collective-permute-start.19 = (f32[3,1,4,128]{3,2,1,0:T(4,128)S(1)}, f32[3,1,4,128]{3,2,1,0:T(4,128)S(1)}, u32[]{:S(2)}, u32[]{:S(2)}) collective-permute-start(f32[3,1,4,128]{3,2,1,0:T(4,128)S(1)} %get-tuple-element.72), channel_id=1, source_target_pairs={{64,0},{128,64},{192,128},{256,192},{320,256},{384,320},{448,384},... | collective-permute-start | bytes 18440 | tf_op jit(solution)/shard_map/ppermute | solution.py:24
  150.5 8.3 %collective-permute-start.20 = (f32[3,6,1,128]{3,2,1,0:T(1,128)S(1)}, f32[3,6,1,128]{3,2,1,0:T(1,128)S(1)}, u32[]{:S(2)}, u32[]{:S(2)}) collective-permute-start(f32[3,6,1,128]{3,2,1,0:T(1,128)S(1)} %get-tuple-element.63), channel_id=1, source_target_pairs={{0,4},{4,8},{8,12},{12,16},{16,20},{20,24},{24,28},{28,32},{32,36}... | collective-permute-start | bytes 27656 | tf_op jit(solution)/shard_map/ppermute | solution.py:22
  152.4 6.4 %collective-permute-start.21 = (f32[3,6,1,128]{3,2,1,0:T(1,128)S(1)}, f32[3,6,1,128]{3,2,1,0:T(1,128)S(1)}, u32[]{:S(2)}, u32[]{:S(2)}) collective-permute-start(f32[3,6,1,128]{3,2,1,0:T(1,128)S(1)} %get-tuple-element.64), channel_id=1, source_target_pairs={{4,0},{8,4},{12,8},{16,12},{20,16},{24,20},{28,24},{32,28},{36,32}... | collective-permute-start | bytes 27656 | tf_op jit(solution)/shard_map/ppermute | solution.py:24
  162.5 6.2 %collective-permute-start.23 = (f32[3,6,6,1]{3,2,1,0:T(8,128)S(1)}, f32[3,6,6,1]{3,2,1,0:T(8,128)S(1)}, u32[]{:S(2)}, u32[]{:S(2)}) collective-permute-start(f32[3,6,6,1]{3,2,1,0:T(8,128)S(1)} %get-tuple-element.55), channel_id=1, source_target_pairs={{1,0},{2,1},{3,2},{5,4},{6,5},{7,6},{9,8},{10,9},{11,10},{13,12},{... | collective-permute-start | bytes 1304 | tf_op jit(solution)/shard_map/ppermute | solution.py:24
  172.1 16.3 %collective-permute-start.25 = (f32[3,1,2,64]{3,2,1,0:T(2,128)S(1)}, f32[3,1,2,64]{3,2,1,0:T(2,128)S(1)}, u32[]{:S(2)}, u32[]{:S(2)}) collective-permute-start(f32[3,1,2,64]{3,2,1,0:T(2,128)S(1)} %get-tuple-element.88), channel_id=1, source_target_pairs={{64,0},{128,64},{192,128},{256,192},{320,256},{384,320},{448,384},... | collective-permute-start | bytes 4616 | tf_op jit(solution)/shard_map/ppermute | solution.py:24
  188.5 7.0 %collective-permute-start.26 = (f32[3,4,1,64]{3,2,1,0:T(1,128)S(1)}, f32[3,4,1,64]{3,2,1,0:T(1,128)S(1)}, u32[]{:S(2)}, u32[]{:S(2)}) collective-permute-start(f32[3,4,1,64]{3,2,1,0:T(1,128)S(1)} %get-tuple-element.83), channel_id=1, source_target_pairs={{0,4},{4,8},{8,12},{12,16},{16,20},{20,24},{24,28},{28,32},{32,36}... | collective-permute-start | bytes 9224 | tf_op jit(solution)/shard_map/ppermute | solution.py:22
  208.0 16.3 %collective-permute-start.31 = (f32[3,1,2,64]{3,2,1,0:T(2,128)S(1)}, f32[3,1,2,64]{3,2,1,0:T(2,128)S(1)}, u32[]{:S(2)}, u32[]{:S(2)}) collective-permute-start(f32[3,1,2,64]{3,2,1,0:T(2,128)S(1)} %get-tuple-element.86), channel_id=1, source_target_pairs={{64,0},{128,64},{192,128},{256,192},{320,256},{384,320},{448,384},... | collective-permute-start | bytes 4616 | tf_op jit(solution)/shard_map/ppermute | solution.py:24
  224.3 7.8 %collective-permute-start.32 = (f32[3,4,1,64]{3,2,1,0:T(1,128)S(1)}, f32[3,4,1,64]{3,2,1,0:T(1,128)S(1)}, u32[]{:S(2)}, u32[]{:S(2)}) collective-permute-start(f32[3,4,1,64]{3,2,1,0:T(1,128)S(1)} %get-tuple-element.81), channel_id=1, source_target_pairs={{0,4},{4,8},{8,12},{12,16},{16,20},{20,24},{24,28},{28,32},{32,36}... | collective-permute-start | bytes 9224 | tf_op jit(solution)/shard_map/ppermute | solution.py:22
  243.0 16.3 %collective-permute-start.37 = (f32[3,1,1,32]{3,2,1,0:T(1,128)S(1)}, f32[3,1,1,32]{3,2,1,0:T(1,128)S(1)}, u32[]{:S(2)}, u32[]{:S(2)}) collective-permute-start(f32[3,1,1,32]{3,2,1,0:T(1,128)S(1)} %get-tuple-element.12), channel_id=1, source_target_pairs={{64,0},{128,64},{192,128},{256,192},{320,256},{384,320},{448,384},... | collective-permute-start | bytes 1160 | tf_op jit(solution)/shard_map/ppermute | solution.py:24
  259.3 6.8 %collective-permute-start.38 = (f32[3,3,1,32]{3,2,1,0:T(1,128)S(1)}, f32[3,3,1,32]{3,2,1,0:T(1,128)S(1)}, u32[]{:S(2)}, u32[]{:S(2)}) collective-permute-start(f32[3,3,1,32]{3,2,1,0:T(1,128)S(1)} %pad_maximum_fusion.115), channel_id=1, source_target_pairs={{0,4},{4,8},{8,12},{12,16},{16,20},{20,24},{24,28},{28,32},{32,36}... | collective-permute-start | bytes 3464 | tf_op jit(solution)/shard_map/ppermute | solution.py:22
  277.1 16.3 %collective-permute-start.43 = (f32[3,1,1,32]{3,2,1,0:T(1,128)S(1)}, f32[3,1,1,32]{3,2,1,0:T(1,128)S(1)}, u32[]{:S(2)}, u32[]{:S(2)}) collective-permute-start(f32[3,1,1,32]{3,2,1,0:T(1,128)S(1)} %divide_add_fusion.4), channel_id=1, source_target_pairs={{64,0},{128,64},{192,128},{256,192},{320,256},{384,320},{448,384},... | collective-permute-start | bytes 1160 | tf_op jit(solution)/shard_map/ppermute | solution.py:24
  293.5 6.8 %collective-permute-start.44 = (f32[3,3,1,32]{3,2,1,0:T(1,128)S(1)}, f32[3,3,1,32]{3,2,1,0:T(1,128)S(1)}, u32[]{:S(2)}, u32[]{:S(2)}) collective-permute-start(f32[3,3,1,32]{3,2,1,0:T(1,128)S(1)} %pad_maximum_fusion.116), channel_id=1, source_target_pairs={{0,4},{4,8},{8,12},{12,16},{16,20},{20,24},{24,28},{28,32},{32,36}... | collective-permute-start | bytes 3464 | tf_op jit(solution)/shard_map/ppermute | solution.py:22
  311.3 16.3 %collective-permute-start.49 = (f32[3,1,1,32]{3,2,1,0:T(1,128)S(1)}, f32[3,1,1,32]{3,2,1,0:T(1,128)S(1)}, u32[]{:S(2)}, u32[]{:S(2)}) collective-permute-start(f32[3,1,1,32]{3,2,1,0:T(1,128)S(1)} %divide_add_fusion.3), channel_id=1, source_target_pairs={{64,0},{128,64},{192,128},{256,192},{320,256},{384,320},{448,384},... | collective-permute-start | bytes 1160 | tf_op jit(solution)/shard_map/ppermute | solution.py:24
  327.6 6.8 %collective-permute-start.50 = (f32[3,3,1,32]{3,2,1,0:T(1,128)S(1)}, f32[3,3,1,32]{3,2,1,0:T(1,128)S(1)}, u32[]{:S(2)}, u32[]{:S(2)}) collective-permute-start(f32[3,3,1,32]{3,2,1,0:T(1,128)S(1)} %pad_maximum_fusion.117), channel_id=1, source_target_pairs={{0,4},{4,8},{8,12},{12,16},{16,20},{20,24},{24,28},{28,32},{32,36}... | collective-permute-start | bytes 3464 | tf_op jit(solution)/shard_map/ppermute | solution.py:22
  (25 other events, 202.4 us)
where the time goes:
time: 358 us; the launch traced here: 356 us
  starting transfers between devices  172 us (48%)
  waiting for transfers between devices  149 us (42%)
  local copies, waits for them, and re-layouts  16.2 us (5%)
  blocking collectives  11.9 us (3%)
  other arithmetic  5.02 us (1%)
    ppermute x27, waiting for transfers between devices, with_halo(): lax.ppermute(head, axis, [((i + 1) % count, i) for i in range(ends)])  145 us
    ppermute x27, starting transfers between devices, with_halo(): lax.ppermute(head, axis, [((i + 1) % count, i) for i in range(ends)])  86.6 us
    ppermute x27, starting transfers between devices, with_halo(): lax.ppermute(tail, axis, [(i, (i + 1) % count) for i in range(ends)])  85.8 us
    slice x64, local copies, waits for them, and re-layouts, every_other(): return lax.slice_in_dim(values, which, values.shape[axis], 2, axis)  12.9 us
    all_gather x1, blocking collectives, local(): coarse_correction = lax.all_gather(own_part, 'gz', axis=3, tiled=True)  11.9 us
  transfers between devices with their start and end apart: 54, of which 33 were waited for; matrix products, arithmetic and copies ran while one was open for 3% of the time, Pallas kernels for 0%

commit v1 on v0

v1 whole, which is shorter than its diff:
```python
import functools

import jax
import jax.numpy as jnp
from jax import lax
from jax.experimental import pallas as pl
from jax.experimental.pallas import tpu as pltpu
from jax.sharding import PartitionSpec as P

MESH = pl.DeviceIdType.MESH
FIELDS = 3
MASS = 0.05
DAMPING = 0.7
DECAY = 0.3
XREACH = 4
YREACH = 3
WIDE = 256


def rs(x, k):
    k %= x.shape[-2]
    return pltpu.roll(x, k, x.ndim - 2) if k else x


def rl(x, k):
    k %= x.shape[-1]
    return pltpu.roll(x, k, x.ndim - 1) if k else x


def harmonic(a, b):
    return 2.0 * a * b / (a + b)


def safe(d):
    return jnp.where(d > 0.0, d, 1.0)


def kernel(names, sizes, phase, conc, pot, src, factor, lev_out, coarse_out, *scratch):
    (ph, co, po, so, in_sem, ys1, yr1, zs1, zr1, xs1, xr1, xs2, xr2, ys3, yr3, zs3, zr3, ys4, yr4, zs4, zr4,
     qb, ys6, yr6, zs6, zr6, ys7, yr7, zs7, zr7, gb, ssem, rsem) = scratch
    ax, ay, az = names
    nx, ny, nz = sizes
    gx, gy, gz = (lax.axis_index(a) for a in names)
    here = {ax: gx, ay: gy, az: gz}
    count = {ax: nx, ay: ny, az: nz}

    def has(axis, step):
        at = here[axis] + step
        return (at >= 0) & (at < count[axis])

    barrier = pltpu.get_barrier_semaphore()
    greet = [(ax, d) for d in range(-XREACH, XREACH + 1) if d] + [(ay, d) for d in range(-YREACH, YREACH + 1) if d]
    met = jnp.int32(nz - 1)
    for axis, d in greet:
        met = met + has(axis, d).astype(jnp.int32)

        @pl.when(has(axis, d))
        def _(axis=axis, d=d):
            pl.semaphore_signal(barrier, inc=1, device_id={axis: here[axis] + d}, device_id_type=MESH)

    for rel in range(1, nz):
        pl.semaphore_signal(barrier, inc=1, device_id={az: lax.rem(gz + rel, nz)}, device_id_type=MESH)

    loads = [pltpu.make_async_copy(a, b, in_sem.at[i]) for i, (a, b) in enumerate(((phase, ph), (conc, co), (pot, po), (src, so)))]
    for load in loads:
        load.start()

    for axis, bufs in ((ax, (xr1, xr2)), (ay, (yr1, yr3, yr4, yr6, yr7)), (az, (zr1, zr3, zr4, zr6, zr7))):
        for side, d in ((0, -1), (1, 1)):

            @pl.when(jnp.logical_not(has(axis, d)))
            def _(bufs=bufs, side=side):
                for buf in bufs:
                    buf[side] = jnp.zeros(buf.shape[1:], jnp.float32)

    for axis, buf, reach in ((ax, qb, XREACH), (ay, gb, YREACH)):
        for d in range(-reach, reach + 1):
            if d:

                @pl.when(jnp.logical_not(has(axis, d)))
                def _(buf=buf, slot=reach + d):
                    buf[slot] = jnp.zeros(buf.shape[1:], jnp.float32)

    pending = []
    used = [0]

    def copy(k, a, b, target):
        return pltpu.make_async_remote_copy(
            src_ref=a, dst_ref=b, send_sem=ssem.at[k], recv_sem=rsem.at[k], device_id=target, device_id_type=MESH
        )

    def push(k, a, b, axis, d):
        pending.append((k, a, b, axis, d))

        @pl.when(has(axis, d))
        def _():
            copy(k, a, b, {axis: here[axis] + d}).start()

    def take(k, b, axis, d):
        @pl.when(has(axis, d))
        def _():
            copy(k, b, b, {axis: here[axis] + d}).wait_recv()

    def exchange(axis, sent, got):
        k = used[0]
        used[0] += 2
        push(k, sent.at[0], got.at[1], axis, -1)
        push(k + 1, sent.at[1], got.at[0], axis, 1)

        def wait():
            take(k, got.at[1], axis, 1)
            take(k + 1, got.at[0], axis, -1)

        return wait

    sub = lax.broadcasted_iota(jnp.int32, (8, WIDE), 0)
    lane = lax.broadcasted_iota(jnp.int32, (8, WIDE), 1)
    lane1 = lax.broadcasted_iota(jnp.int32, (8, 128), 1)

    def zpack(sent, slabs, stride, unit):
        low = high = jnp.zeros((8, 128), jnp.float32)
        for k, s in enumerate(slabs):
            mine = (lane1 >= unit * k) & (lane1 < unit * (k + 1))
            low = jnp.where(mine, rl(s[:, :128], unit * k), low)
            high = jnp.where(mine, rl(s[:, 128:], unit * k - (128 - stride)), high)
        sent[0] = low
        sent[1] = high

    def zhalo(low, high, k, stride, unit):
        return jnp.concatenate([rl(low, -unit * k), rl(high, 128 - stride - unit * k)], axis=1)

    def ypack_rows(sent, slabs, stride):
        for g in range(sent.shape[1]):
            low = high = jnp.zeros((8, WIDE), jnp.float32)
            for j, s in enumerate(slabs[8 * g : 8 * g + 8]):
                low = jnp.where(sub == j, rs(s, j), low)
                high = jnp.where(sub == j, rs(s, j - (8 - stride)), high)
            sent[0, g] = low
            sent[1, g] = high

    def row(got, side, k):
        return jnp.broadcast_to(got[side, k // 8, k % 8 : k % 8 + 1, :], (8, WIDE))

    loads[0].wait()
    loads[1].wait()
    loads[2].wait()
    phase_v = ph[...]
    conc_v = co[...]
    lookup = jnp.zeros(phase_v.shape, jnp.float32)
    for i in range(3):
        lookup = lookup + jnp.where(phase_v == i, factor[i], 0.0)
    conduct = lookup * conc_v * jnp.exp(-DECAY * conc_v)
    fine = [jnp.stack([conduct[x]] + [po[f, x] for f in range(FIELDS)]) for x in range(8)]
    ypack_rows(ys1, [fine[x][a] for a in range(4) for x in range(8)], 1)
    zpack(zs1, [fine[x][a] for a in range(4) for x in range(8)], 1, 1)
    xs1[0] = fine[0]
    xs1[1] = fine[7]
    loads[3].wait()

    pl.semaphore_wait(barrier, met)

    wait_y1 = exchange(ay, ys1, yr1)
    wait_z1 = exchange(az, zs1, zr1)
    wait_x1 = exchange(ax, xs1, xr1)

    def rest(c):
        return c[0], c[1:]

    def flux(c, v, other):
        face = harmonic(c, other[0])
        return face, face * (v - other[1:])

    inner = []
    for i in range(3):
        a, b = fine[2 * i + 1], fine[2 * i + 2]
        inner.append(flux(a[0], a[1:], b))

    wait_y1()
    wait_z1()
    zlow, zhigh = zr1[0], zr1[1]
    part, ypart, zpart = [], [], []
    for x in range(8):
        c, v = rest(fine[x])
        near = jnp.where(sub % 2 == 0, rs(fine[x], 1), rs(fine[x], -1))
        edge = jnp.stack([jnp.where(sub == 0, row(yr1, 0, a * 8 + x), row(yr1, 1, a * 8 + x)) for a in range(4)])
        near = jnp.where((sub == 0) | (sub == 7), edge, near)
        sy, fy = flux(c, v, near)
        near = jnp.where(lane % 2 == 0, rl(fine[x], 1), rl(fine[x], -1))
        edge = jnp.stack([zhalo(zlow, zhigh, a * 8 + x, 1, 1) for a in range(4)])
        near = jnp.where((lane == 0) | (lane == WIDE - 1), edge, near)
        sz, fz = flux(c, v, near)
        source = jnp.stack([so[f, x] for f in range(FIELDS)])
        part.append(source - MASS * v - fy - fz)
        ypart.append(sy)
        zpart.append(sz)

    def fold(t, stride):
        t = t + rl(t, -stride)
        return t + rs(t, -stride)

    mass1 = MASS * 8.0
    r1, ylo, yhi, zlo, zhi, diag, sx = {}, {}, {}, {}, {}, {}, {}
    for i in range(3):
        sx[i] = fold(inner[i][0], 1)
    for i in range(4):
        t = part[2 * i] + part[2 * i + 1]
        if i < 3:
            t = t - inner[i][1]
        if i > 0:
            t = t + inner[i - 1][1]
        r1[i] = fold(t, 1)
        a = ypart[2 * i] + ypart[2 * i + 1]
        a = a + rl(a, -1)
        ylo[i], yhi[i] = a, rs(a, -1)
        b = zpart[2 * i] + zpart[2 * i + 1]
        b = b + rs(b, -1)
        zlo[i], zhi[i] = b, rl(b, -1)
        d = mass1 + ylo[i] + yhi[i] + zlo[i] + zhi[i]
        if i < 3:
            d = d + sx[i]
        if i > 0:
            d = d + sx[i - 1]
        diag[i] = d

    e0, weight = {}, {}
    for i in (1, 2):
        weight[i] = DAMPING / safe(diag[i])
        e0[i] = weight[i] * r1[i]

    q0 = sub % 2 == 0
    p0 = lane % 2 == 0

    def merge4(a, b, c, d):
        return jnp.where(q0, jnp.where(p0, a, rl(b, 1)), jnp.where(p0, rs(c, 1), rs(rl(d, 1), 1)))

    def split4(m):
        low = rs(m, -1)
        return m, rl(m, -1), low, rl(low, -1)

    for side, (edge, next_to, face) in enumerate(((0, 1, 0), (3, 2, 2))):
        xs2[side, 0] = merge4(e0[next_to][0], e0[next_to][1], e0[next_to][2], diag[edge])
        xs2[side, 1] = merge4(r1[edge][0], r1[edge][1], r1[edge][2], sx[face])
        xs2[side, 2] = merge4(ylo[edge], yhi[edge], zlo[edge], zhi[edge])
    wait_x2 = exchange(ax, xs2, xr2)

    wait_x1()
    border = {}
    for side, x in ((0, 0), (1, 7)):
        face, out = flux(fine[x][0], fine[x][1:], xr1[side])
        border[side] = (fold(face, 1), fold(out, 1))
    wait_x2()
    for side, edge, out, far, own_face, far_face in ((0, 0, -1, -2, -1, -2), (1, 3, 4, 5, 3, 4)):
        face, through = border[side]
        a = split4(xr2[side, 0])
        b = split4(xr2[side, 1])
        c = split4(xr2[side, 2])
        e0[far] = jnp.stack(a[:3])
        r1[out] = jnp.stack(b[:3]) + through
        r1[edge] = r1[edge] - through
        sx[far_face] = b[3]
        sx[own_face] = face
        ylo[out], yhi[out], zlo[out], zhi[out] = c
        diag[out] = a[3] + face
        diag[edge] = diag[edge] + face
        for i in (out, edge):
            weight[i] = DAMPING / safe(diag[i])
            e0[i] = weight[i] * r1[i]

    def halos(got_y, got_z, layers, low, high, i):
        base = layers.index(i) * FIELDS
        ylow = jnp.stack([row(got_y, 0, base + f) for f in range(FIELDS)])
        yhigh = jnp.stack([row(got_y, 1, base + f) for f in range(FIELDS)])
        zedge = jnp.stack([zhalo(low, high, base + f, 2, 1) for f in range(FIELDS)])
        return ylow, yhigh, zedge

    six = [-1, 0, 1, 2, 3, 4]
    slabs = [e0[i][f] for i in six for f in range(FIELDS)]
    ypack_rows(ys3, slabs, 2)
    wait_y = exchange(ay, ys3, yr3)
    zpack(zs3, slabs, 2, 1)
    wait_z = exchange(az, zs3, zr3)
    wait_y()
    wait_z()
    low, high = zr3[0], zr3[1]
    e1 = {}
    for i in six:
        e = e0[i]
        ylow, yhigh, zedge = halos(yr3, zr3, six, low, high, i)
        total = mass1 * e + sx[i - 1] * (e - e0[i - 1]) + sx[i] * (e - e0[i + 1])
        total = total + ylo[i] * (e - jnp.where(sub < 2, ylow, rs(e, 2)))
        total = total + yhi[i] * (e - jnp.where(sub >= 6, yhigh, rs(e, -2)))
        total = total + zlo[i] * (e - jnp.where(lane < 2, zedge, rl(e, 2)))
        total = total + zhi[i] * (e - jnp.where(lane >= WIDE - 2, zedge, rl(e, -2)))
        e1[i] = e + weight[i] * (r1[i] - total)

    four = [0, 1, 2, 3]
    slabs = [e1[i][f] for i in four for f in range(FIELDS)]
    ypack_rows(ys4, slabs, 2)
    wait_y = exchange(ay, ys4, yr4)
    zpack(zs4, slabs, 2, 1)
    wait_z = exchange(az, zs4, zr4)

    mass2 = mass1 * 8.0
    yfirst = sub % 4 < 2
    zfirst = lane % 4 < 2
    yout = {i: jnp.where(yfirst, ylo[i], yhi[i]) for i in four}
    zout = {i: jnp.where(zfirst, zlo[i], zhi[i]) for i in four}
    sx2 = {-1: fold(sx[-1], 2), 0: fold(sx[1], 2), 1: fold(sx[3], 2)}
    ylo2, yhi2, zlo2, zhi2, diag2 = {}, {}, {}, {}, {}
    for i in range(2):
        a = yout[2 * i] + yout[2 * i + 1]
        a = a + rl(a, -2)
        ylo2[i], yhi2[i] = a, rs(a, -2)
        b = zout[2 * i] + zout[2 * i + 1]
        b = b + rs(b, -2)
        zlo2[i], zhi2[i] = b, rl(b, -2)
        diag2[i] = mass2 + sx2[i - 1] + sx2[i] + ylo2[i] + yhi2[i] + zlo2[i] + zhi2[i]

    wait_y()
    wait_z()
    low, high = zr4[0], zr4[1]
    left = {}
    for i in four:
        e = e1[i]
        ylow, yhigh, zedge = halos(yr4, zr4, four, low, high, i)
        across = i - 1 if i % 2 == 0 else i + 1
        near_y = jnp.where(yfirst, jnp.where(sub < 2, ylow, rs(e, 2)), jnp.where(sub >= 6, yhigh, rs(e, -2)))
        near_z = jnp.where(zfirst, rl(e, 2), rl(e, -2))
        near_z = jnp.where((lane < 2) | (lane >= WIDE - 2), zedge, near_z)
        total = mass1 * e + sx[min(i, across)] * (e - e1[across])
        total = total + yout[i] * (e - near_y) + zout[i] * (e - near_z)
        left[i] = r1[i] - total
    r2 = {i: fold(left[2 * i] + left[2 * i + 1], 2) for i in range(2)}

    q4 = sub % 4
    p4 = lane % 4

    def by(which, a, b, c, d):
        return jnp.where(which < 2, jnp.where(which == 0, a, b), jnp.where(which == 2, c, d))

    def rows4(a, b, c, d):
        return by(q4, a, rs(b, 1), rs(c, 2), rs(d, 3))

    block = by(
        p4,
        rows4(r2[0][0], r2[0][1], r2[0][2], diag2[0]),
        rl(rows4(r2[1][0], r2[1][1], r2[1][2], diag2[1]), 1),
        rl(rows4(sx2[0], yhi2[0], zhi2[0], zlo2[0]), 2),
        rl(rows4(sx2[1], yhi2[1], zhi2[1], zlo2[1]), 3),
    )
    qb[XREACH] = block
    first = used[0]
    steps = [d for d in range(-XREACH, XREACH + 1) if d]
    used[0] += len(steps)
    for k, d in enumerate(steps):
        push(first + k, qb.at[XREACH], qb.at[XREACH - d], ax, d)

    packed = jnp.concatenate([merge4(*(e1[i][f] for i in four)) for f in range(FIELDS)], axis=0)
    r = lax.broadcasted_iota(jnp.int32, (WIDE, WIDE), 0)
    c = lax.broadcasted_iota(jnp.int32, (WIDE, WIDE), 1)
    order = jnp.where(c == (r % 2) * 128 + r // 2, 1.0, 0.0)
    dense = jnp.dot(packed, order, precision=lax.Precision.HIGHEST, preferred_element_type=jnp.float32)
    for f in range(FIELDS):
        for y in range(4):
            for q in range(2):
                for p in range(2):
                    k = f * 8 + 2 * y + q
                    lev_out[f, 2 * q + p, y : y + 1, :] = dense[k : k + 1, 128 * p : 128 * p + 128]

    for k, d in enumerate(steps):
        take(first + k, qb.at[XREACH - d], ax, -d)

    n2 = 2 * XREACH + 1
    q = qb[...]

    def spread(x, item):
        return jnp.where(q4 == 0, rs(x, -item), jnp.where(q4 == 1, rs(x, 1 - item), rs(x, 2 - item)))

    layer0 = p4 == 0
    weight2 = DAMPING / safe(spread(q, 3))
    coef = rl(q, -2)
    xhi, yhi_, zhi_, zlo_ = (spread(coef, item) for item in range(4))
    e = weight2 * q

    def below(x):
        return jnp.concatenate([x[:1], x[:-1]], axis=0)

    def above(x):
        return jnp.concatenate([x[1:], x[-1:]], axis=0)

    def next_x(x):
        return jnp.where(layer0, rl(x, -1), above(rl(x, 1)))

    def last_x(x):
        return jnp.where(layer0, below(rl(x, -1)), rl(x, 1))

    def ypack_halves(sent, x):
        for g in range(sent.shape[1]):
            a, b = x[2 * g], x[min(2 * g + 1, x.shape[0] - 1)]
            sent[0, g] = jnp.where(sub < 4, a, rs(b, 4))
            sent[1, g] = jnp.where(sub < 4, rs(a, 4), b)

    def yedges(got, n):
        out = []
        for d in range(n):
            low, high = got[0, d // 2], got[1, d // 2]
            if d % 2 == 0:
                out.append(jnp.where(sub < 4, low, rs(high, 4)))
            else:
                out.append(jnp.where(sub < 4, rs(low, 4), high))
        return jnp.stack(out)

    def zedges(got, n):
        low, high = got[0], got[1]
        return jnp.stack([zhalo(low, high, d, 4, 4) for d in range(n)])

    ypack_halves(ys6, jnp.where(q4 == 3, rs(coef, 2), e))
    wait_y = exchange(ay, ys6, yr6)
    zpack(zs6, [e[d] for d in range(n2)], 4, 4)
    wait_z = exchange(az, zs6, zr6)
    xlo = last_x(xhi)
    near = xlo * (e - last_x(e)) + xhi * (e - next_x(e)) + mass2 * e
    wait_y()
    wait_z()
    edge = yedges(yr6, n2)
    zedge = zedges(zr6, n2)
    ylo_ = jnp.where(sub < 4, spread(edge, 3), rs(yhi_, 4))
    other = rs(e, 4)
    total = near + ylo_ * (e - jnp.where(sub < 4, edge, other)) + yhi_ * (e - jnp.where(sub < 4, other, edge))
    total = total + zlo_ * (e - jnp.where(lane < 4, zedge, rl(e, 4)))
    total = total + zhi_ * (e - jnp.where(lane >= WIDE - 4, zedge, rl(e, -4)))
    e = e + weight2 * (q - total)

    n3 = n2 - 2
    ypack_halves(ys7, e[1:-1])
    wait_y = exchange(ay, ys7, yr7)
    zpack(zs7, [e[d] for d in range(1, n2 - 1)], 4, 4)
    wait_z = exchange(az, zs7, zr7)

    mass3 = mass2 * 8.0
    zfirst = lane % 8 < 4
    xout = jnp.where(layer0, xlo, xhi)[1:-1]
    yout = jnp.where(sub < 4, ylo_, yhi_)[1:-1]
    zout = jnp.where(zfirst, zlo_, zhi_)[1:-1]
    a = xout + rs(xout, 4)
    a = a + rl(a, -4)
    xlo3, xhi3 = a, rl(a, -1)
    a = yout + rl(yout, -1)
    a = a + rl(a, -4)
    ylo3, yhi3 = a, rs(a, 4)
    a = zout + rl(zout, -1)
    a = a + rs(a, 4)
    zlo3, zhi3 = a, rl(a, -4)
    diag3 = mass3 + xlo3 + xhi3 + ylo3 + yhi3 + zlo3 + zhi3
    near_x = jnp.where(layer0, last_x(e), next_x(e))[1:-1]
    e = e[1:-1]
    near_z = jnp.where(zfirst, rl(e, 4), rl(e, -4))
    partial = q[1:-1] - mass2 * e - xout * (e - near_x)
    coefs = jnp.where(sub == 3, rs(diag3, 3), jnp.where(sub == 4, rs(xhi3, 4), jnp.where(sub == 5, rs(yhi3, 5), rs(zhi3, 6))))
    wait_y()
    wait_z()
    edge = yedges(yr7, n3)
    zedge = zedges(zr7, n3)
    near_z = jnp.where((lane < 4) | (lane >= WIDE - 4), zedge, near_z)
    t = partial - yout * (e - edge) - zout * (e - near_z)
    t = t + rl(t, -1)
    t = t + rs(t, 4)
    t = t + rl(t, -4)
    t = jnp.where(sub < 3, t, coefs)
    block = jnp.zeros((8, WIDE), jnp.float32)
    for l in range(n3):
        block = jnp.where((lane % 8 == l) & (sub < 7), rl(t[l], l), block)

    def column(at):
        return gb.at[YREACH, :, pl.ds(pl.multiple_of(at * WIDE, WIDE), WIDE)]

    gb[YREACH, :, pl.ds(pl.multiple_of(gz * WIDE, WIDE), WIDE)] = block
    first = used[0]
    used[0] += nz - 1
    along = []
    for rel in range(1, nz):
        c = copy(first + rel - 1, column(gz), column(gz), {az: lax.rem(gz + rel, nz)})
        c.start()
        along.append(c)
    for rel in range(1, nz):
        back = lax.rem(gz + nz - rel, nz)
        copy(first + rel - 1, column(back), column(back), {az: back}).wait_recv()
    first = used[0]
    steps = [d for d in range(-YREACH, YREACH + 1) if d]
    used[0] += len(steps)
    for k, d in enumerate(steps):
        push(first + k, gb.at[YREACH], gb.at[YREACH - d], ay, d)
    for k, d in enumerate(steps):
        take(first + k, gb.at[YREACH - d], ay, -d)

    full = (8, WIDE * nz)
    n = 2 * YREACH + 1

    def coefficient(j, item):
        return jnp.broadcast_to(gb[j, item : item + 1, :], full)

    r3 = [gb[j] for j in range(n)]
    w3 = [DAMPING / safe(coefficient(j, 3)) for j in range(n)]
    e = {j: w3[j] * r3[j] for j in range(n)}
    xhi = {j: coefficient(j, 4) for j in range(1, n - 1)}
    yhi = {j: coefficient(j, 5) for j in range(n - 1)}
    zhi = {j: coefficient(j, 6) for j in range(1, n - 1)}
    xlo = {j: rl(xhi[j], 1) for j in xhi}
    zlo = {j: rl(zhi[j], 8) for j in zhi}
    for sweep in range(1, YREACH + 1):
        new = {}
        for j in range(sweep, n - sweep):
            v = e[j]
            total = mass3 * v + xlo[j] * (v - rl(v, 1)) + xhi[j] * (v - rl(v, -1))
            total = total + yhi[j - 1] * (v - e[j - 1]) + yhi[j] * (v - e[j + 1])
            total = total + zlo[j] * (v - rl(v, 8)) + zhi[j] * (v - rl(v, -8))
            new[j] = v + w3[j] * (r3[j] - total)
        e = new
    own = e[YREACH]
    tile = jnp.zeros((8, 128), jnp.float32)
    for t in range(2 * nz):
        tile = jnp.where(lane1 % 8 == t, rl(own[:, 128 * t : 128 * t + 128], t - XREACH + 1), tile)
    r = lax.broadcasted_iota(jnp.int32, (128, 32 * nz), 0)
    c = lax.broadcasted_iota(jnp.int32, (128, 32 * nz), 1)
    order = jnp.where(c == (r % 8) * 16 + r // 8, 1.0, 0.0)
    dense = jnp.dot(tile, order, precision=lax.Precision.HIGHEST, preferred_element_type=jnp.float32)
    for f in range(FIELDS):
        coarse_out[f, 0, :, :] = dense[f : f + 1, :]

    for k, a, b, axis, d in pending:

        @pl.when(has(axis, d))
        def _(k=k, a=a, b=b, axis=axis, d=d):
            copy(k, a, b, {axis: here[axis] + d}).wait_send()

    for c in along:
        c.wait_send()


def solution(mesh):
    names = mesh.axis_names
    sizes = tuple(mesh.shape[a] for a in names)
    nz = sizes[2]
    f32 = jnp.float32

    def both(*shape):
        return [pltpu.VMEM((2, *shape), f32)] * 2

    scratch = [
        pltpu.VMEM((8, 8, WIDE), jnp.int32),
        pltpu.VMEM((8, 8, WIDE), f32),
        pltpu.VMEM((FIELDS, 8, 8, WIDE), f32),
        pltpu.VMEM((FIELDS, 8, 8, WIDE), f32),
        pltpu.SemaphoreType.DMA((4,)),
        *both(4, 8, WIDE), *both(8, 128), *both(4, 8, WIDE), *both(3, 8, WIDE),
        *both(3, 8, WIDE), *both(8, 128),
        *both(2, 8, WIDE), *both(8, 128),
        pltpu.VMEM((2 * XREACH + 1, 8, WIDE), f32),
        *both(5, 8, WIDE), *both(8, 128),
        *both(4, 8, WIDE), *both(8, 128),
        pltpu.VMEM((2 * YREACH + 1, 8, WIDE * nz), f32),
    ]
    sems = 2 * 4 + 4 + 4 + 2 * XREACH + 4 + 4 + (nz - 1) + 2 * YREACH
    scratch += [pltpu.SemaphoreType.DMA((sems,)), pltpu.SemaphoreType.DMA((sems,))]

    def local(phase_label, concentration, phase_factor, potential, source):
        return pl.pallas_call(
            functools.partial(kernel, names, sizes),
            out_shape=(
                jax.ShapeDtypeStruct((FIELDS, 4, 4, 128), f32),
                jax.ShapeDtypeStruct((FIELDS, 1, 1, 32 * nz), f32),
            ),
            in_specs=[pl.BlockSpec(memory_space=pl.ANY)] * 4 + [pl.BlockSpec(memory_space=pltpu.SMEM)],
            out_specs=(pl.BlockSpec(memory_space=pltpu.VMEM), pl.BlockSpec(memory_space=pltpu.VMEM)),
            scratch_shapes=scratch,
            compiler_params=pltpu.CompilerParams(collective_id=0, has_side_effects=True, vmem_limit_bytes=32 << 20),
        )(phase_label, concentration, potential, source, phase_factor)

    return jax.shard_map(
        local,
        mesh=mesh,
        in_specs=(P(*names), P(*names), P(), P(None, *names), P(None, *names)),
        out_specs=(P(None, *names), P(None, names[0], names[1], None)),
        check_vma=False,
    )
```

time: 358 us -> 73.1 us (0.20)
  the two profiles are of different devices: /device:TPU:134 before, /device:TPU:263 now
where the time goes in v1:
time: 73.1 us; the launch traced here: 72.8 us
  Pallas kernels  66.8 us (91%)
  local copies, waits for them, and re-layouts  5.35 us (7%)
    pallas_call x1, Pallas kernels, local(): pl.pallas_call(functools.partial(kernel, names, sizes), out_shape=(jax.Sh...  66.8 us
    unnamed x12, local copies, waits for them, and re-layouts  5.35 us

profile of v1, /device:TPU:263, one launch (start us, length us, event | category | flops | bytes accessed | tf_op | source)
XLA Modules:
  0.0 72.8 jit_solution(2662114590251636795)
XLA Ops:
  0.6 0.0 copy-start
  0.6 0.9 %copy-done = f32[3,8,8,256]{3,2,1,0:T(8,128)S(1)} copy-done((f32[3,8,8,256]{3,2,1,0:T(8,128)S(1)}, f32[3,8,8,256]{3,2,1,0:T(8,128)}, u32[]{:S(2)}) %copy-start) | copy-done | bytes 196632
  1.6 0.0 copy-start.1
  1.6 0.9 %copy-done.1 = f32[3,8,8,256]{3,2,1,0:T(8,128)S(1)} copy-done((f32[3,8,8,256]{3,2,1,0:T(8,128)S(1)}, f32[3,8,8,256]{3,2,1,0:T(8,128)}, u32[]{:S(2)}) %copy-start.1) | copy-done | bytes 196632
  2.5 0.0 copy-start.2
  2.5 0.8 %copy-done.2 = s32[8,8,256]{2,1,0:T(8,128)S(1)} copy-done((s32[8,8,256]{2,1,0:T(8,128)S(1)}, s32[8,8,256]{2,1,0:T(8,128)}, u32[]{:S(2)}) %copy-start.2) | copy-done | bytes 65560
  3.3 0.0 copy-start.3
  3.3 0.8 %copy-done.3 = f32[8,8,256]{2,1,0:T(8,128)S(1)} copy-done((f32[8,8,256]{2,1,0:T(8,128)S(1)}, f32[8,8,256]{2,1,0:T(8,128)}, u32[]{:S(2)}) %copy-start.3) | copy-done | bytes 65560
  4.2 0.0 copy-start.4
  4.2 0.7 copy-done.4
  4.8 66.8 %shard_map.68 = (f32[3,4,4,128]{3,2,1,0:T(4,128)S(1)}, f32[3,1,1,128]{3,2,1,0:T(1,128)S(1)}) custom-call(s32[8,8,256]{2,1,0:T(8,128)S(1)} %copy-done.2, f32[8,8,256]{2,1,0:T(8,128)S(1)} %copy-done.3, f32[3,8,8,256]{3,2,1,0:T(8,128)S(1)} %copy-done, f32[3,8,8,256]{3,2,1,0:T(8,128)S(1)} %copy-done.1, f32[3]{0:T(128)S(1)} %copy-done.4), custom_call_target="tpu_custom_call" | custom-call | tf_op jit(solution)/shard_map/pallas_call | solution.py:567
  71.6 0.6 copy.9
  72.3 0.6 copy.10
Async XLA Ops:
  0.6 0.9 %copy-start = (f32[3,8,8,256]{3,2,1,0:T(8,128)S(1)}, f32[3,8,8,256]{3,2,1,0:T(8,128)}, u32[]{:S(2)}) copy-start(f32[3,8,8,256]{3,2,1,0:T(8,128)} %pot.1) | copy-start | bytes 589828
  1.6 0.9 %copy-start.1 = (f32[3,8,8,256]{3,2,1,0:T(8,128)S(1)}, f32[3,8,8,256]{3,2,1,0:T(8,128)}, u32[]{:S(2)}) copy-start(f32[3,8,8,256]{3,2,1,0:T(8,128)} %src.1) | copy-start | bytes 589828
  2.5 0.8 %copy-start.2 = (s32[8,8,256]{2,1,0:T(8,128)S(1)}, s32[8,8,256]{2,1,0:T(8,128)}, u32[]{:S(2)}) copy-start(s32[8,8,256]{2,1,0:T(8,128)} %phase.1) | copy-start | bytes 196612
  3.3 0.8 %copy-start.3 = (f32[8,8,256]{2,1,0:T(8,128)S(1)}, f32[8,8,256]{2,1,0:T(8,128)}, u32[]{:S(2)}) copy-start(f32[8,8,256]{2,1,0:T(8,128)} %conc.1) | copy-start | bytes 196612
  4.2 0.7 copy-start.4

commit v2 on v1

--- a/solution.py
+++ b/solution.py
@@ -15,6 +15,7 @@
 XREACH = 4
 YREACH = 3
 WIDE = 256
+XROW = 4
 
 
 def rs(x, k):
@@ -35,9 +36,9 @@
     return jnp.where(d > 0.0, d, 1.0)
 
 
-def kernel(names, sizes, phase, conc, pot, src, factor, lev_out, coarse_out, *scratch):
-    (ph, co, po, so, in_sem, ys1, yr1, zs1, zr1, xs1, xr1, xs2, xr2, ys3, yr3, zs3, zr3, ys4, yr4, zs4, zr4,
-     qb, ys6, yr6, zs6, zr6, ys7, yr7, zs7, zr7, gb, ssem, rsem) = scratch
+def kernel(names, sizes, phase, conc, pot, src, factors, lev_out, coarse_out, *scratch):
+    (ph, co, po, so, in_sem, ys1, yr1, zs1, zr1, xs1, xr1, xk1, xs2, xr2, xk2, ys3, yr3, zs3, zr3, ys4, yr4, zs4, zr4,
+     qb, ys6, yr6, zs6, zr6, ys7, yr7, zs7, zr7, gb, factor, ssem, rsem) = scratch
     ax, ay, az = names
     nx, ny, nz = sizes
     gx, gy, gz = (lax.axis_index(a) for a in names)
@@ -49,19 +50,29 @@
         return (at >= 0) & (at < count[axis])
 
     barrier = pltpu.get_barrier_semaphore()
-    greet = [(ax, d) for d in range(-XREACH, XREACH + 1) if d] + [(ay, d) for d in range(-YREACH, YREACH + 1) if d]
     met = jnp.int32(nz - 1)
-    for axis, d in greet:
-        met = met + has(axis, d).astype(jnp.int32)
-
-        @pl.when(has(axis, d))
-        def _(axis=axis, d=d):
-            pl.semaphore_signal(barrier, inc=1, device_id={axis: here[axis] + d}, device_id_type=MESH)
+    for d in range(-XREACH, XREACH + 1):
+        if d:
+            met = met + has(ax, d).astype(jnp.int32)
+
+            @pl.when(has(ax, d))
+            def _(d=d):
+                pl.semaphore_signal(barrier, inc=1, device_id={ax: gx + d}, device_id_type=MESH)
+
+    for d in range(-YREACH, YREACH + 1):
+        if d:
+            met = met + nz * has(ay, d).astype(jnp.int32)
+
+            @pl.when(has(ay, d))
+            def _(d=d):
+                for rel in range(nz):
+                    to = {ay: gy + d, az: lax.rem(gz + rel, nz)}
+                    pl.semaphore_signal(barrier, inc=1, device_id=to, device_id_type=MESH)
 
     for rel in range(1, nz):
         pl.semaphore_signal(barrier, inc=1, device_id={az: lax.rem(gz + rel, nz)}, device_id_type=MESH)
 
-    loads = [pltpu.make_async_copy(a, b, in_sem.at[i]) for i, (a, b) in enumerate(((phase, ph), (conc, co), (pot, po), (src, so)))]
+    loads = [pltpu.make_async_copy(a, b, in_sem.at[i]) for i, (a, b) in enumerate(((phase, ph), (conc, co), (factors, factor), (pot, po), (src, so)))]
     for load in loads:
         load.start()
 
@@ -84,26 +95,35 @@
     pending = []
     used = [0]
 
+    def fresh(n=1):
+        used[0] += n
+        return used[0] - n
+
     def copy(k, a, b, target):
         return pltpu.make_async_remote_copy(
             src_ref=a, dst_ref=b, send_sem=ssem.at[k], recv_sem=rsem.at[k], device_id=target, device_id_type=MESH
         )
 
+    def start(k, a, b, target, when):
+        pending.append((k, a, b, target, when))
+
+        @pl.when(when)
+        def _():
+            copy(k, a, b, target).start()
+
+    def arrived(k, b, when):
+        @pl.when(when)
+        def _():
+            copy(k, b, b, {}).wait_recv()
+
     def push(k, a, b, axis, d):
-        pending.append((k, a, b, axis, d))
-
-        @pl.when(has(axis, d))
-        def _():
-            copy(k, a, b, {axis: here[axis] + d}).start()
+        start(k, a, b, {axis: here[axis] + d}, has(axis, d))
 
     def take(k, b, axis, d):
-        @pl.when(has(axis, d))
-        def _():
-            copy(k, b, b, {axis: here[axis] + d}).wait_recv()
+        arrived(k, b, has(axis, d))
 
     def exchange(axis, sent, got):
-        k = used[0]
-        used[0] += 2
+        k = fresh(2)
         push(k, sent.at[0], got.at[1], axis, -1)
         push(k + 1, sent.at[1], got.at[0], axis, 1)
 
@@ -112,6 +132,50 @@
             take(k + 1, got.at[0], axis, -1)
 
         return wait
+
+    place = lax.rem(gx, XROW)
+
+    class Crossing:
+        def __init__(self, sent, got, kept, pieces, lines):
+            self.sent, self.got, self.kept, self.pieces, self.lines = sent, got, kept, pieces, lines
+            self.whole = fresh(2)
+            self.part = fresh(2 * len(pieces))
+            self.hop = fresh(2 * len(pieces))
+            for side, d in ((0, -1), (1, 1)):
+                edge = 0 if side == 0 else XROW - 1
+                inside = has(ax, d) & (place != edge)
+                leaves = has(ax, d) & (place == edge)
+                start(self.whole + side, sent.at[side], got.at[1 - side], {ax: gx + d}, inside)
+                for i, piece in enumerate(pieces):
+                    line = lines[side][i]
+                    if line == edge:
+                        start(self.sem(side, i), sent.at[side, piece], got.at[1 - side, piece], {ax: gx + d}, leaves)
+                    else:
+                        peer = {ax: gx + line - edge}
+                        k = self.hop + side * len(pieces) + i
+                        start(k, sent.at[side, piece], kept.at[side], peer, leaves)
+
+        def sem(self, side, i):
+            return self.part + side * len(self.pieces) + i
+
+        def forward(self):
+            for side, d in ((0, -1), (1, 1)):
+                edge = 0 if side == 0 else XROW - 1
+                to = gx - place + edge + d
+                exists = (to >= 0) & (to < nx)
+                for i, piece in enumerate(self.pieces):
+                    line = self.lines[side][i]
+                    if line != edge:
+                        mine = exists & (place == line)
+                        arrived(self.hop + side * len(self.pieces) + i, self.kept.at[side], mine)
+                        start(self.sem(side, i), self.kept.at[side], self.got.at[1 - side, piece], {ax: to}, mine)
+
+        def finish(self):
+            for side, d in ((0, -1), (1, 1)):
+                edge = 0 if side == 0 else XROW - 1
+                arrived(self.whole + 1 - side, self.got.at[side], has(ax, d) & (place != edge))
+                for i, piece in enumerate(self.pieces):
+                    arrived(self.sem(1 - side, i), self.got.at[side, piece], has(ax, d) & (place == edge))
 
     sub = lax.broadcasted_iota(jnp.int32, (8, WIDE), 0)
     lane = lax.broadcasted_iota(jnp.int32, (8, WIDE), 1)
@@ -144,6 +208,7 @@
     loads[0].wait()
     loads[1].wait()
     loads[2].wait()
+    loads[3].wait()
     phase_v = ph[...]
     conc_v = co[...]
     lookup = jnp.zeros(phase_v.shape, jnp.float32)
@@ -155,13 +220,14 @@
     zpack(zs1, [fine[x][a] for a in range(4) for x in range(8)], 1, 1)
     xs1[0] = fine[0]
     xs1[1] = fine[7]
-    loads[3].wait()
+    loads[4].wait()
 
     pl.semaphore_wait(barrier, met)
 
     wait_y1 = exchange(ay, ys1, yr1)
     wait_z1 = exchange(az, zs1, zr1)
-    wait_x1 = exchange(ax, xs1, xr1)
+    slabs = [pl.ds(i, 1) for i in range(4)]
+    early = Crossing(xs1, xr1, xk1, slabs, ([0, 1, 2, 3], [0, 1, 2, 3]))
 
     def rest(c):
         return c[0], c[1:]
@@ -241,14 +307,15 @@
         xs2[side, 0] = merge4(e0[next_to][0], e0[next_to][1], e0[next_to][2], diag[edge])
         xs2[side, 1] = merge4(r1[edge][0], r1[edge][1], r1[edge][2], sx[face])
         xs2[side, 2] = merge4(ylo[edge], yhi[edge], zlo[edge], zhi[edge])
-    wait_x2 = exchange(ax, xs2, xr2)
-
-    wait_x1()
+    late = Crossing(xs2, xr2, xk2, [pl.ds(0, 2), pl.ds(2, 1)], ([0, 1], [XROW - 1, XROW - 2]))
+    early.forward()
+    late.forward()
+    early.finish()
     border = {}
     for side, x in ((0, 0), (1, 7)):
         face, out = flux(fine[x][0], fine[x][1:], xr1[side])
         border[side] = (fold(face, 1), fold(out, 1))
-    wait_x2()
+    late.finish()
     for side, edge, out, far, own_face, far_face in ((0, 0, -1, -2, -1, -2), (1, 3, 4, 5, 3, 4)):
         face, through = border[side]
         a = split4(xr2[side, 0])
@@ -349,11 +416,10 @@
         rl(rows4(sx2[1], yhi2[1], zhi2[1], zlo2[1]), 3),
     )
     qb[XREACH] = block
-    first = used[0]
-    steps = [d for d in range(-XREACH, XREACH + 1) if d]
-    used[0] += len(steps)
-    for k, d in enumerate(steps):
-        push(first + k, qb.at[XREACH], qb.at[XREACH - d], ax, d)
+    direct = fresh(2 * XREACH + 1)
+    for d in (-XREACH, XREACH, 1, -1, 2, -2, 3, -3):
+        inside = has(ax, d) if abs(d) == XREACH else has(ax, d) & (place + d >= 0) & (place + d < XROW)
+        start(direct + XREACH - d, qb.at[XREACH], qb.at[XREACH - d], {ax: gx + d}, inside)
 
     packed = jnp.concatenate([merge4(*(e1[i][f] for i in four)) for f in range(FIELDS)], axis=0)
     r = lax.broadcasted_iota(jnp.int32, (WIDE, WIDE), 0)
@@ -367,8 +433,20 @@
                     k = f * 8 + 2 * y + q
                     lev_out[f, 2 * q + p, y : y + 1, :] = dense[k : k + 1, 128 * p : 128 * p + 128]
 
-    for k, d in enumerate(steps):
-        take(first + k, qb.at[XREACH - d], ax, -d)
+    handed = fresh(2 * XREACH + 1)
+    for side in (-1, 1):
+        far = XREACH + side * XREACH
+        take(direct + far, qb.at[far], ax, side * XREACH)
+        for step in range(1, XROW):
+            slot = far - side * step
+            inside = has(ax, side * XREACH) & (place + side * step >= 0) & (place + side * step < XROW)
+            start(handed + slot, qb.at[far], qb.at[slot], {ax: gx + side * step}, inside)
+    for side in (-1, 1):
+        for step in range(1, XROW):
+            slot = XREACH + side * step
+            inside = (place + side * step >= 0) & (place + side * step < XROW)
+            arrived(direct + slot, qb.at[slot], has(ax, side * step) & inside)
+            arrived(handed + slot, qb.at[slot], has(ax, side * step) & jnp.logical_not(inside))
 
     n2 = 2 * XREACH + 1
     q = qb[...]
@@ -471,27 +549,19 @@
     for l in range(n3):
         block = jnp.where((lane % 8 == l) & (sub < 7), rl(t[l], l), block)
 
-    def column(at):
-        return gb.at[YREACH, :, pl.ds(pl.multiple_of(at * WIDE, WIDE), WIDE)]
+    def column(slot, at):
+        return gb.at[slot, :, pl.ds(pl.multiple_of(at * WIDE, WIDE), WIDE)]
 
     gb[YREACH, :, pl.ds(pl.multiple_of(gz * WIDE, WIDE), WIDE)] = block
-    first = used[0]
-    used[0] += nz - 1
-    along = []
-    for rel in range(1, nz):
-        c = copy(first + rel - 1, column(gz), column(gz), {az: lax.rem(gz + rel, nz)})
-        c.start()
-        along.append(c)
-    for rel in range(1, nz):
-        back = lax.rem(gz + nz - rel, nz)
-        copy(first + rel - 1, column(back), column(back), {az: back}).wait_recv()
-    first = used[0]
-    steps = [d for d in range(-YREACH, YREACH + 1) if d]
-    used[0] += len(steps)
-    for k, d in enumerate(steps):
-        push(first + k, gb.at[YREACH], gb.at[YREACH - d], ay, d)
-    for k, d in enumerate(steps):
-        take(first + k, gb.at[YREACH - d], ay, -d)
+    first = fresh((2 * YREACH + 1) * nz)
+    others = [(d, rel) for d in sorted(range(-YREACH, YREACH + 1), key=abs) for rel in range(nz) if d or rel]
+    for d, rel in others:
+        k = first + (YREACH - d) * nz + rel
+        to = {ay: gy + d, az: lax.rem(gz + rel, nz)}
+        start(k, column(YREACH, gz), column(YREACH - d, gz), to, has(ay, d))
+    for d, rel in others:
+        k = first + (YREACH - d) * nz + rel
+        arrived(k, column(YREACH - d, lax.rem(gz + nz - rel, nz)), has(ay, -d))
 
     full = (8, WIDE * nz)
     n = 2 * YREACH + 1
@@ -527,14 +597,11 @@
     for f in range(FIELDS):
         coarse_out[f, 0, :, :] = dense[f : f + 1, :]
 
-    for k, a, b, axis, d in pending:
-
-        @pl.when(has(axis, d))
-        def _(k=k, a=a, b=b, axis=axis, d=d):
-            copy(k, a, b, {axis: here[axis] + d}).wait_send()
-
-    for c in along:
-        c.wait_send()
+    for k, a, b, target, when in pending:
+
+        @pl.when(when)
+        def _(k=k, a=a, b=b, target=target):
+            copy(k, a, b, target).wait_send()
 
 
 def solution(mesh):
@@ -551,16 +618,18 @@
         pltpu.VMEM((8, 8, WIDE), f32),
         pltpu.VMEM((FIELDS, 8, 8, WIDE), f32),
         pltpu.VMEM((FIELDS, 8, 8, WIDE), f32),
-        pltpu.SemaphoreType.DMA((4,)),
-        *both(4, 8, WIDE), *both(8, 128), *both(4, 8, WIDE), *both(3, 8, WIDE),
+        pltpu.SemaphoreType.DMA((5,)),
+        *both(4, 8, WIDE), *both(8, 128),
+        *both(4, 8, WIDE), pltpu.VMEM((2, 1, 8, WIDE), f32), *both(3, 8, WIDE), pltpu.VMEM((2, 1, 8, WIDE), f32),
         *both(3, 8, WIDE), *both(8, 128),
         *both(2, 8, WIDE), *both(8, 128),
         pltpu.VMEM((2 * XREACH + 1, 8, WIDE), f32),
         *both(5, 8, WIDE), *both(8, 128),
         *both(4, 8, WIDE), *both(8, 128),
         pltpu.VMEM((2 * YREACH + 1, 8, WIDE * nz), f32),
+        pltpu.SMEM((3,), f32),
     ]
-    sems = 2 * 4 + 4 + 4 + 2 * XREACH + 4 + 4 + (nz - 1) + 2 * YREACH
+    sems = 2 * 2 * 5 + (2 + 16) + (2 + 8) + 2 * (2 * XREACH + 1) + (2 * YREACH + 1) * nz
     scratch += [pltpu.SemaphoreType.DMA((sems,)), pltpu.SemaphoreType.DMA((sems,))]
 
     def local(phase_label, concentration, phase_factor, potential, source):
@@ -570,10 +639,10 @@
                 jax.ShapeDtypeStruct((FIELDS, 4, 4, 128), f32),
                 jax.ShapeDtypeStruct((FIELDS, 1, 1, 32 * nz), f32),
             ),
-            in_specs=[pl.BlockSpec(memory_space=pl.ANY)] * 4 + [pl.BlockSpec(memory_space=pltpu.SMEM)],
+            in_specs=[pl.BlockSpec(memory_space=pltpu.HBM)] * 5,
             out_specs=(pl.BlockSpec(memory_space=pltpu.VMEM), pl.BlockSpec(memory_space=pltpu.VMEM)),
             scratch_shapes=scratch,
-            compiler_params=pltpu.CompilerParams(collective_id=0, has_side_effects=True, vmem_limit_bytes=32 << 20),
+            compiler_params=pltpu.CompilerParams(collective_id=0, has_side_effects=True, vmem_limit_bytes=55168 << 10),
         )(phase_label, concentration, potential, source, phase_factor)
 
     return jax.shard_map(

time: 73.1 us -> 68.9 us (0.943)
  the two profiles are of different devices: /device:TPU:263 before, /device:TPU:69 now
where the time goes in v2:
time: 68.9 us; the launch traced here: 68.7 us
  Pallas kernels  66.2 us (96%)
  local copies, waits for them, and re-layouts  1.82 us (3%)
    pallas_call x1, Pallas kernels, local(): pl.pallas_call(functools.partial(kernel, names, sizes), out_shape=(jax.Sh...  66.2 us
    unnamed x4, local copies, waits for them, and re-layouts  1.82 us

profile of v2, /device:TPU:69, one launch (start us, length us, event | category | flops | bytes accessed | tf_op | source)
XLA Modules:
  0.0 68.7 jit_solution(9968242460722661444)
XLA Ops:
  0.6 0.0 copy-start
  0.6 0.6 copy-done
  1.3 66.2 %shard_map.68 = (f32[3,4,4,128]{3,2,1,0:T(4,128)S(1)}, f32[3,1,1,128]{3,2,1,0:T(1,128)S(1)}) custom-call(s32[8,8,256]{2,1,0:T(8,128)} %phase.1, f32[8,8,256]{2,1,0:T(8,128)} %conc.1, f32[3,8,8,256]{3,2,1,0:T(8,128)} %pot.1, f32[3,8,8,256]{3,2,1,0:T(8,128)} %src.1, f32[3]{0:T(128)S(1)} %copy-done), custom_call_target="tpu_custom_call" | custom-call | tf_op jit(solution)/shard_map/pallas_call | solution.py:636
  67.5 0.6 copy.9
  68.1 0.6 copy.10
Async XLA Ops:
  0.6 0.7 copy-start

commit v3 on v2

--- a/solution.py
+++ b/solution.py
@@ -38,7 +38,7 @@
 
 def kernel(names, sizes, phase, conc, pot, src, factors, lev_out, coarse_out, *scratch):
     (ph, co, po, so, in_sem, ys1, yr1, zs1, zr1, xs1, xr1, xk1, xs2, xr2, xk2, ys3, yr3, zs3, zr3, ys4, yr4, zs4, zr4,
-     qb, ys6, yr6, zs6, zr6, ys7, yr7, zs7, zr7, gb, factor, ssem, rsem) = scratch
+     qb, ys6, yr6, zs6, zr6, ys7, yr7, zs7, zr7, gb, factor, row_sem, ssem, rsem) = scratch
     ax, ay, az = names
     nx, ny, nz = sizes
     gx, gy, gz = (lax.axis_index(a) for a in names)
@@ -50,14 +50,17 @@
         return (at >= 0) & (at < count[axis])
 
     barrier = pltpu.get_barrier_semaphore()
+    place = lax.rem(gx, XROW)
     met = jnp.int32(nz - 1)
-    for d in range(-XREACH, XREACH + 1):
-        if d:
-            met = met + has(ax, d).astype(jnp.int32)
-
-            @pl.when(has(ax, d))
-            def _(d=d):
-                pl.semaphore_signal(barrier, inc=1, device_id={ax: gx + d}, device_id_type=MESH)
+    for d in (1, -1, 2, -2, 3, -3):
+        known = has(ax, d) & (place + d >= 0) & (place + d < XROW)
+        if abs(d) == 1:
+            known = has(ax, d)
+        met = met + known.astype(jnp.int32)
+
+        @pl.when(known)
+        def _(d=d):
+            pl.semaphore_signal(barrier, inc=1, device_id={ax: gx + d}, device_id_type=MESH)
 
     for d in range(-YREACH, YREACH + 1):
         if d:
@@ -116,6 +119,15 @@
         def _():
             copy(k, b, b, {}).wait_recv()
 
+    def drain(n):
+        for k, a, b, target, when in pending[:n]:
+
+            @pl.when(when)
+            def _(k=k, a=a, b=b, target=target):
+                copy(k, a, b, target).wait_send()
+
+        del pending[:n]
+
     def push(k, a, b, axis, d):
         start(k, a, b, {axis: here[axis] + d}, has(axis, d))
 
@@ -132,8 +144,6 @@
             take(k + 1, got.at[0], axis, -1)
 
         return wait
-
-    place = lax.rem(gx, XROW)
 
     class Crossing:
         def __init__(self, sent, got, kept, pieces, lines):
@@ -311,6 +321,14 @@
     early.forward()
     late.forward()
     early.finish()
+    for side, edge in ((0, 0), (1, XROW - 1)):
+        step = 1 if side == 0 else -1
+
+        @pl.when((place == edge) & has(ax, -step))
+        def _(side=side, step=step):
+            for i in range(1, XROW):
+                pl.semaphore_signal(row_sem.at[side], inc=1, device_id={ax: gx + step * i}, device_id_type=MESH)
+
     border = {}
     for side, x in ((0, 0), (1, 7)):
         face, out = flux(fine[x][0], fine[x][1:], xr1[side])
@@ -416,11 +434,19 @@
         rl(rows4(sx2[1], yhi2[1], zhi2[1], zlo2[1]), 3),
     )
     qb[XREACH] = block
+    old = len(pending)
     direct = fresh(2 * XREACH + 1)
+    for side, edge in ((0, 0), (1, XROW - 1)):
+
+        @pl.when((place != edge) & has(ax, XREACH * (2 * side - 1)))
+        def _(side=side):
+            pl.semaphore_wait(row_sem.at[side], 1)
+
     for d in (-XREACH, XREACH, 1, -1, 2, -2, 3, -3):
         inside = has(ax, d) if abs(d) == XREACH else has(ax, d) & (place + d >= 0) & (place + d < XROW)
         start(direct + XREACH - d, qb.at[XREACH], qb.at[XREACH - d], {ax: gx + d}, inside)
 
+    drain(old)
     packed = jnp.concatenate([merge4(*(e1[i][f] for i in four)) for f in range(FIELDS)], axis=0)
     r = lax.broadcasted_iota(jnp.int32, (WIDE, WIDE), 0)
     c = lax.broadcasted_iota(jnp.int32, (WIDE, WIDE), 1)
@@ -554,11 +580,13 @@
 
     gb[YREACH, :, pl.ds(pl.multiple_of(gz * WIDE, WIDE), WIDE)] = block
     first = fresh((2 * YREACH + 1) * nz)
+    old = len(pending)
     others = [(d, rel) for d in sorted(range(-YREACH, YREACH + 1), key=abs) for rel in range(nz) if d or rel]
     for d, rel in others:
         k = first + (YREACH - d) * nz + rel
         to = {ay: gy + d, az: lax.rem(gz + rel, nz)}
         start(k, column(YREACH, gz), column(YREACH - d, gz), to, has(ay, d))
+    drain(old)
     for d, rel in others:
         k = first + (YREACH - d) * nz + rel
         arrived(k, column(YREACH - d, lax.rem(gz + nz - rel, nz)), has(ay, -d))
@@ -597,11 +625,7 @@
     for f in range(FIELDS):
         coarse_out[f, 0, :, :] = dense[f : f + 1, :]
 
-    for k, a, b, target, when in pending:
-
-        @pl.when(when)
-        def _(k=k, a=a, b=b, target=target):
-            copy(k, a, b, target).wait_send()
+    drain(len(pending))
 
 
 def solution(mesh):
@@ -630,7 +654,7 @@
         pltpu.SMEM((3,), f32),
     ]
     sems = 2 * 2 * 5 + (2 + 16) + (2 + 8) + 2 * (2 * XREACH + 1) + (2 * YREACH + 1) * nz
-    scratch += [pltpu.SemaphoreType.DMA((sems,)), pltpu.SemaphoreType.DMA((sems,))]
+    scratch += [pltpu.SemaphoreType.REGULAR((2,)), pltpu.SemaphoreType.DMA((sems,)), pltpu.SemaphoreType.DMA((sems,))]
 
     def local(phase_label, concentration, phase_factor, potential, source):
         return pl.pallas_call(

time: 68.9 us -> 67.6 us (0.981)
  Pallas kernels: 66.2 us -> 65 us
    pallas_call x1, Pallas kernels: 66.2 us -> 65 us  [local(): pl.pallas_call(functools.partial(kernel, names, sizes), out_shape=(jax.Sh...]
where the time goes in v3:
time: 67.6 us; the launch traced here: 67.5 us
  Pallas kernels  65 us (96%)
  local copies, waits for them, and re-layouts  1.82 us (3%)
    pallas_call x1, Pallas kernels, local(): pl.pallas_call(functools.partial(kernel, names, sizes), out_shape=(jax.Sh...  65 us
    unnamed x4, local copies, waits for them, and re-layouts  1.82 us

profile of v3, /device:TPU:69, one launch (start us, length us, event | category | flops | bytes accessed | tf_op | source)
XLA Modules:
  0.0 67.5 jit_solution(14746395883807486110)
XLA Ops:
  0.6 0.0 copy-start
  0.6 0.6 copy-done
  1.3 65.0 %shard_map.68 = (f32[3,4,4,128]{3,2,1,0:T(4,128)S(1)}, f32[3,1,1,128]{3,2,1,0:T(1,128)S(1)}) custom-call(s32[8,8,256]{2,1,0:T(8,128)} %phase.1, f32[8,8,256]{2,1,0:T(8,128)} %conc.1, f32[3,8,8,256]{3,2,1,0:T(8,128)} %pot.1, f32[3,8,8,256]{3,2,1,0:T(8,128)} %src.1, f32[3]{0:T(128)S(1)} %copy-done), custom_call_target="tpu_custom_call" | custom-call | tf_op jit(solution)/shard_map/pallas_call | solution.py:660
  66.3 0.6 copy.9
  66.9 0.6 copy.10
Async XLA Ops:
  0.6 0.7 copy-start

commit v4 on v3

--- a/solution.py
+++ b/solution.py
@@ -15,6 +15,7 @@
 XREACH = 4
 YREACH = 3
 WIDE = 256
+HALVES = (-3, -2, 2, 3)
 XROW = 4
 
 
@@ -38,7 +39,7 @@
 
 def kernel(names, sizes, phase, conc, pot, src, factors, lev_out, coarse_out, *scratch):
     (ph, co, po, so, in_sem, ys1, yr1, zs1, zr1, xs1, xr1, xk1, xs2, xr2, xk2, ys3, yr3, zs3, zr3, ys4, yr4, zs4, zr4,
-     qb, ys6, yr6, zs6, zr6, ys7, yr7, zs7, zr7, gb, factor, row_sem, ssem, rsem) = scratch
+     qb, ys6, yr6, zs6, zr6, ys7, yr7, zs7, zr7, gb, gh, hs, factor, row_sem, ssem, rsem) = scratch
     ax, ay, az = names
     nx, ny, nz = sizes
     gx, gy, gz = (lax.axis_index(a) for a in names)
@@ -87,13 +88,13 @@
                 for buf in bufs:
                     buf[side] = jnp.zeros(buf.shape[1:], jnp.float32)
 
-    for axis, buf, reach in ((ax, qb, XREACH), (ay, gb, YREACH)):
-        for d in range(-reach, reach + 1):
-            if d:
-
-                @pl.when(jnp.logical_not(has(axis, d)))
-                def _(buf=buf, slot=reach + d):
-                    buf[slot] = jnp.zeros(buf.shape[1:], jnp.float32)
+    blocks = [(ax, d, qb, XREACH + d) for d in range(-XREACH, XREACH + 1) if d]
+    blocks += [(ay, d, gb, YREACH + d) for d in (-1, 1)] + [(ay, d, gh, i) for i, d in enumerate(HALVES)]
+    for axis, d, buf, slot in blocks:
+
+        @pl.when(jnp.logical_not(has(axis, d)))
+        def _(buf=buf, slot=slot):
+            buf[slot] = jnp.zeros(buf.shape[1:], jnp.float32)
 
     pending = []
     used = [0]
@@ -353,14 +354,17 @@
 
     def halos(got_y, got_z, layers, low, high, i):
         base = layers.index(i) * FIELDS
-        ylow = jnp.stack([row(got_y, 0, base + f) for f in range(FIELDS)])
-        yhigh = jnp.stack([row(got_y, 1, base + f) for f in range(FIELDS)])
+        ylow = jnp.stack([rl(row(got_y, 0, k // 2), -(k % 2)) for k in range(base, base + FIELDS)])
+        yhigh = jnp.stack([rl(row(got_y, 1, k // 2), -(k % 2)) for k in range(base, base + FIELDS)])
         zedge = jnp.stack([zhalo(low, high, base + f, 2, 1) for f in range(FIELDS)])
         return ylow, yhigh, zedge
 
+    def two_by_two(slabs):
+        return [jnp.where(p0, a, rl(b, 1)) for a, b in zip(slabs[::2], slabs[1::2])]
+
     six = [-1, 0, 1, 2, 3, 4]
     slabs = [e0[i][f] for i in six for f in range(FIELDS)]
-    ypack_rows(ys3, slabs, 2)
+    ypack_rows(ys3, two_by_two(slabs), 2)
     wait_y = exchange(ay, ys3, yr3)
     zpack(zs3, slabs, 2, 1)
     wait_z = exchange(az, zs3, zr3)
@@ -380,7 +384,7 @@
 
     four = [0, 1, 2, 3]
     slabs = [e1[i][f] for i in four for f in range(FIELDS)]
-    ypack_rows(ys4, slabs, 2)
+    ypack_rows(ys4, two_by_two(slabs), 2)
     wait_y = exchange(ay, ys4, yr4)
     zpack(zs4, slabs, 2, 1)
     wait_z = exchange(az, zs4, zr4)
@@ -499,15 +503,19 @@
         return jnp.where(layer0, below(rl(x, -1)), rl(x, 1))
 
     def ypack_halves(sent, x):
-        for g in range(sent.shape[1]):
-            a, b = x[2 * g], x[min(2 * g + 1, x.shape[0] - 1)]
-            sent[0, g] = jnp.where(sub < 4, a, rs(b, 4))
-            sent[1, g] = jnp.where(sub < 4, rs(a, 4), b)
+        low, high = [], []
+        for m in range(0, x.shape[0], 2):
+            a, b = x[m], x[min(m + 1, x.shape[0] - 1)]
+            low.append(jnp.where(sub < 4, a, rs(b, 4)))
+            high.append(jnp.where(sub < 4, rs(a, 4), b))
+        for side, h in ((0, low), (1, high)):
+            for g in range(sent.shape[1]):
+                sent[side, g] = jnp.where(p4 < 2, h[2 * g], rl(h[min(2 * g + 1, len(h) - 1)], 2))
 
     def yedges(got, n):
         out = []
         for d in range(n):
-            low, high = got[0, d // 2], got[1, d // 2]
+            low, high = (rl(got[side, d // 4], -2 * (d // 2 % 2)) for side in (0, 1))
             if d % 2 == 0:
                 out.append(jnp.where(sub < 4, low, rs(high, 4)))
             else:
@@ -578,18 +586,33 @@
     def column(slot, at):
         return gb.at[slot, :, pl.ds(pl.multiple_of(at * WIDE, WIDE), WIDE)]
 
+    def half(slot, at):
+        return gh.at[slot, :, pl.ds(pl.multiple_of(at * 128, 128), 128)]
+
     gb[YREACH, :, pl.ds(pl.multiple_of(gz * WIDE, WIDE), WIDE)] = block
+    third = lane1 % 8
+    hs[...] = jnp.where(third < 3, rl(block[:, :128], -2), jnp.where(third < 6, rl(block[:, 128:], 1), 0.0))
     first = fresh((2 * YREACH + 1) * nz)
     old = len(pending)
     others = [(d, rel) for d in sorted(range(-YREACH, YREACH + 1), key=abs) for rel in range(nz) if d or rel]
     for d, rel in others:
         k = first + (YREACH - d) * nz + rel
         to = {ay: gy + d, az: lax.rem(gz + rel, nz)}
-        start(k, column(YREACH, gz), column(YREACH - d, gz), to, has(ay, d))
+        if d in HALVES:
+            start(k, hs, half(HALVES.index(-d), gz), to, has(ay, d))
+        else:
+            start(k, column(YREACH, gz), column(YREACH - d, gz), to, has(ay, d))
     drain(old)
     for d, rel in others:
         k = first + (YREACH - d) * nz + rel
-        arrived(k, column(YREACH - d, lax.rem(gz + nz - rel, nz)), has(ay, -d))
+        back = lax.rem(gz + nz - rel, nz)
+        arrived(k, half(HALVES.index(-d), back) if d in HALVES else column(YREACH - d, back), has(ay, -d))
+    middle = (third >= 2) & (third < 5)
+    for i, d in enumerate(HALVES):
+        for at in range(nz):
+            m = gh[i, :, 128 * at : 128 * at + 128]
+            gb[YREACH + d, :, WIDE * at : WIDE * at + 128] = jnp.where(middle, rl(m, 2), 0.0)
+            gb[YREACH + d, :, WIDE * at + 128 : WIDE * at + 256] = jnp.where(middle, rl(m, -1), 0.0)
 
     full = (8, WIDE * nz)
     n = 2 * YREACH + 1
@@ -645,12 +668,14 @@
         pltpu.SemaphoreType.DMA((5,)),
         *both(4, 8, WIDE), *both(8, 128),
         *both(4, 8, WIDE), pltpu.VMEM((2, 1, 8, WIDE), f32), *both(3, 8, WIDE), pltpu.VMEM((2, 1, 8, WIDE), f32),
+        *both(2, 8, WIDE), *both(8, 128),
+        *both(1, 8, WIDE), *both(8, 128),
+        pltpu.VMEM((2 * XREACH + 1, 8, WIDE), f32),
         *both(3, 8, WIDE), *both(8, 128),
         *both(2, 8, WIDE), *both(8, 128),
-        pltpu.VMEM((2 * XREACH + 1, 8, WIDE), f32),
-        *both(5, 8, WIDE), *both(8, 128),
-        *both(4, 8, WIDE), *both(8, 128),
         pltpu.VMEM((2 * YREACH + 1, 8, WIDE * nz), f32),
+        pltpu.VMEM((len(HALVES), 8, 128 * nz), f32),
+        pltpu.VMEM((8, 128), f32),
         pltpu.SMEM((3,), f32),
     ]
     sems = 2 * 2 * 5 + (2 + 16) + (2 + 8) + 2 * (2 * XREACH + 1) + (2 * YREACH + 1) * nz

time: 67.6 us -> 67.3 us (level)
  no operation moved by 1% of the time
where the time goes in v4:
time: 67.3 us; the launch traced here: 67.1 us
  Pallas kernels  64.6 us (96%)
  local copies, waits for them, and re-layouts  1.82 us (3%)
    pallas_call x1, Pallas kernels, local(): pl.pallas_call(functools.partial(kernel, names, sizes), out_shape=(jax.Sh...  64.6 us
    unnamed x4, local copies, waits for them, and re-layouts  1.82 us

profile of v4, /device:TPU:69, one launch (start us, length us, event | category | flops | bytes accessed | tf_op | source)
XLA Modules:
  0.0 67.1 jit_solution(15598241611753687427)
XLA Ops:
  0.6 0.0 copy-start
  0.6 0.6 copy-done
  1.3 64.6 %shard_map.68 = (f32[3,4,4,128]{3,2,1,0:T(4,128)S(1)}, f32[3,1,1,128]{3,2,1,0:T(1,128)S(1)}) custom-call(s32[8,8,256]{2,1,0:T(8,128)} %phase.1, f32[8,8,256]{2,1,0:T(8,128)} %conc.1, f32[3,8,8,256]{3,2,1,0:T(8,128)} %pot.1, f32[3,8,8,256]{3,2,1,0:T(8,128)} %src.1, f32[3]{0:T(128)S(1)} %copy-done), custom_call_target="tpu_custom_call" | custom-call | tf_op jit(solution)/shard_map/pallas_call | solution.py:685
  65.9 0.6 copy.9
  66.5 0.6 copy.10
Async XLA Ops:
  0.6 0.7 copy-start

commit v5 on v4

--- a/solution.py
+++ b/solution.py
@@ -46,9 +46,13 @@
     here = {ax: gx, ay: gy, az: gz}
     count = {ax: nx, ay: ny, az: nz}
 
+    known_steps = {}
+
     def has(axis, step):
-        at = here[axis] + step
-        return (at >= 0) & (at < count[axis])
+        if (axis, step) not in known_steps:
+            at = here[axis] + step
+            known_steps[axis, step] = (at >= 0) & (at < count[axis])
+        return known_steps[axis, step]
 
     barrier = pltpu.get_barrier_semaphore()
     place = lax.rem(gx, XROW)
@@ -108,32 +112,38 @@
             src_ref=a, dst_ref=b, send_sem=ssem.at[k], recv_sem=rsem.at[k], device_id=target, device_id_type=MESH
         )
 
-    def start(k, a, b, target, when):
-        pending.append((k, a, b, target, when))
+    def start(copies, when):
+        pending.append((copies, when))
 
         @pl.when(when)
         def _():
-            copy(k, a, b, target).start()
-
-    def arrived(k, b, when):
+            for c in copies:
+                copy(*c).start()
+
+    def arrived(copies, when):
         @pl.when(when)
         def _():
-            copy(k, b, b, {}).wait_recv()
+            for k, b in copies:
+                copy(k, b, b, {}).wait_recv()
 
     def drain(n):
-        for k, a, b, target, when in pending[:n]:
+        groups = {}
+        for copies, when in pending[:n]:
+            groups.setdefault(id(when), (when, []))[1].extend(copies)
+        for when, copies in groups.values():
 
             @pl.when(when)
-            def _(k=k, a=a, b=b, target=target):
-                copy(k, a, b, target).wait_send()
+            def _(copies=copies):
+                for c in copies:
+                    copy(*c).wait_send()
 
         del pending[:n]
 
     def push(k, a, b, axis, d):
-        start(k, a, b, {axis: here[axis] + d}, has(axis, d))
+        start([(k, a, b, {axis: here[axis] + d})], has(axis, d))
 
     def take(k, b, axis, d):
-        arrived(k, b, has(axis, d))
+        arrived([(k, b)], has(axis, d))
 
     def exchange(axis, sent, got):
         k = fresh(2)
@@ -156,15 +166,16 @@
                 edge = 0 if side == 0 else XROW - 1
                 inside = has(ax, d) & (place != edge)
                 leaves = has(ax, d) & (place == edge)
-                start(self.whole + side, sent.at[side], got.at[1 - side], {ax: gx + d}, inside)
+                start([(self.whole + side, sent.at[side], got.at[1 - side], {ax: gx + d})], inside)
+                copies = []
                 for i, piece in enumerate(pieces):
                     line = lines[side][i]
                     if line == edge:
-                        start(self.sem(side, i), sent.at[side, piece], got.at[1 - side, piece], {ax: gx + d}, leaves)
+                        copies.append((self.sem(side, i), sent.at[side, piece], got.at[1 - side, piece], {ax: gx + d}))
                     else:
-                        peer = {ax: gx + line - edge}
                         k = self.hop + side * len(pieces) + i
-                        start(k, sent.at[side, piece], kept.at[side], peer, leaves)
+                        copies.append((k, sent.at[side, piece], kept.at[side], {ax: gx + line - edge}))
+                start(copies, leaves)
 
         def sem(self, side, i):
             return self.part + side * len(self.pieces) + i
@@ -178,15 +189,15 @@
                     line = self.lines[side][i]
                     if line != edge:
                         mine = exists & (place == line)
-                        arrived(self.hop + side * len(self.pieces) + i, self.kept.at[side], mine)
-                        start(self.sem(side, i), self.kept.at[side], self.got.at[1 - side, piece], {ax: to}, mine)
+                        arrived([(self.hop + side * len(self.pieces) + i, self.kept.at[side])], mine)
+                        start([(self.sem(side, i), self.kept.at[side], self.got.at[1 - side, piece], {ax: to})], mine)
 
         def finish(self):
             for side, d in ((0, -1), (1, 1)):
                 edge = 0 if side == 0 else XROW - 1
-                arrived(self.whole + 1 - side, self.got.at[side], has(ax, d) & (place != edge))
-                for i, piece in enumerate(self.pieces):
-                    arrived(self.sem(1 - side, i), self.got.at[side, piece], has(ax, d) & (place == edge))
+                arrived([(self.whole + 1 - side, self.got.at[side])], has(ax, d) & (place != edge))
+                parts = [(self.sem(1 - side, i), self.got.at[side, piece]) for i, piece in enumerate(self.pieces)]
+                arrived(parts, has(ax, d) & (place == edge))
 
     sub = lax.broadcasted_iota(jnp.int32, (8, WIDE), 0)
     lane = lax.broadcasted_iota(jnp.int32, (8, WIDE), 1)
@@ -448,7 +459,7 @@
 
     for d in (-XREACH, XREACH, 1, -1, 2, -2, 3, -3):
         inside = has(ax, d) if abs(d) == XREACH else has(ax, d) & (place + d >= 0) & (place + d < XROW)
-        start(direct + XREACH - d, qb.at[XREACH], qb.at[XREACH - d], {ax: gx + d}, inside)
+        start([(direct + XREACH - d, qb.at[XREACH], qb.at[XREACH - d], {ax: gx + d})], inside)
 
     drain(old)
     packed = jnp.concatenate([merge4(*(e1[i][f] for i in four)) for f in range(FIELDS)], axis=0)
@@ -470,13 +481,13 @@
         for step in range(1, XROW):
             slot = far - side * step
             inside = has(ax, side * XREACH) & (place + side * step >= 0) & (place + side * step < XROW)
-            start(handed + slot, qb.at[far], qb.at[slot], {ax: gx + side * step}, inside)
+            start([(handed + slot, qb.at[far], qb.at[slot], {ax: gx + side * step})], inside)
     for side in (-1, 1):
         for step in range(1, XROW):
             slot = XREACH + side * step
             inside = (place + side * step >= 0) & (place + side * step < XROW)
-            arrived(direct + slot, qb.at[slot], has(ax, side * step) & inside)
-            arrived(handed + slot, qb.at[slot], has(ax, side * step) & jnp.logical_not(inside))
+            arrived([(direct + slot, qb.at[slot])], has(ax, side * step) & inside)
+            arrived([(handed + slot, qb.at[slot])], has(ax, side * step) & jnp.logical_not(inside))
 
     n2 = 2 * XREACH + 1
     q = qb[...]
@@ -594,19 +605,22 @@
     hs[...] = jnp.where(third < 3, rl(block[:, :128], -2), jnp.where(third < 6, rl(block[:, 128:], 1), 0.0))
     first = fresh((2 * YREACH + 1) * nz)
     old = len(pending)
-    others = [(d, rel) for d in sorted(range(-YREACH, YREACH + 1), key=abs) for rel in range(nz) if d or rel]
-    for d, rel in others:
-        k = first + (YREACH - d) * nz + rel
-        to = {ay: gy + d, az: lax.rem(gz + rel, nz)}
-        if d in HALVES:
-            start(k, hs, half(HALVES.index(-d), gz), to, has(ay, d))
-        else:
-            start(k, column(YREACH, gz), column(YREACH - d, gz), to, has(ay, d))
+    order3 = [(d, [rel for rel in (2, 1, 3, 0) if rel < nz and (d or rel)]) for d in (3, -3, 2, -2, 1, -1, 0)]
+    order3 = [(d, rels) for d, rels in order3 if rels]
+
+    def place3(d, at):
+        return half(HALVES.index(d), at) if d in HALVES else column(YREACH + d, at)
+
+    def sem3(d, rel):
+        return first + (YREACH - d) * nz + rel
+
+    for d, rels in order3:
+        source = hs if d in HALVES else column(YREACH, gz)
+        to = [{ay: gy + d, az: lax.rem(gz + rel, nz)} for rel in rels]
+        start([(sem3(d, rel), source, place3(-d, gz), t) for rel, t in zip(rels, to)], has(ay, d))
     drain(old)
-    for d, rel in others:
-        k = first + (YREACH - d) * nz + rel
-        back = lax.rem(gz + nz - rel, nz)
-        arrived(k, half(HALVES.index(-d), back) if d in HALVES else column(YREACH - d, back), has(ay, -d))
+    for d, rels in reversed(order3):
+        arrived([(sem3(d, rel), place3(-d, lax.rem(gz + nz - rel, nz))) for rel in rels], has(ay, -d))
     middle = (third >= 2) & (third < 5)
     for i, d in enumerate(HALVES):
         for at in range(nz):

time: 67.3 us -> 66.6 us (0.990)
  no operation moved by 1% of the time
where the time goes in v5:
time: 66.6 us; the launch traced here: 66.5 us
  Pallas kernels  64 us (96%)
  local copies, waits for them, and re-layouts  1.82 us (3%)
    pallas_call x1, Pallas kernels, local(): pl.pallas_call(functools.partial(kernel, names, sizes), out_shape=(jax.Sh...  64 us
    unnamed x4, local copies, waits for them, and re-layouts  1.82 us

profile of v5, /device:TPU:69, one launch (start us, length us, event | category | flops | bytes accessed | tf_op | source)
XLA Modules:
  0.0 66.5 jit_solution(5883000437940811319)
XLA Ops:
  0.6 0.0 copy-start
  0.6 0.6 copy-done
  1.3 64.0 %shard_map.68 = (f32[3,4,4,128]{3,2,1,0:T(4,128)S(1)}, f32[3,1,1,128]{3,2,1,0:T(1,128)S(1)}) custom-call(s32[8,8,256]{2,1,0:T(8,128)} %phase.1, f32[8,8,256]{2,1,0:T(8,128)} %conc.1, f32[3,8,8,256]{3,2,1,0:T(8,128)} %pot.1, f32[3,8,8,256]{3,2,1,0:T(8,128)} %src.1, f32[3]{0:T(128)S(1)} %copy-done), custom_call_target="tpu_custom_call" | custom-call | tf_op jit(solution)/shard_map/pallas_call | solution.py:699
  65.3 0.6 copy.9
  65.9 0.6 copy.10
Async XLA Ops:
  0.6 0.7 copy-start

commit v6 on v5

--- a/solution.py
+++ b/solution.py
@@ -67,6 +67,10 @@
         def _(d=d):
             pl.semaphore_signal(barrier, inc=1, device_id={ax: gx + d}, device_id_type=MESH)
 
+    loads = [pltpu.make_async_copy(a, b, in_sem.at[i]) for i, (a, b) in enumerate(((phase, ph), (conc, co), (factors, factor), (pot, po), (src, so)))]
+    for load in loads:
+        load.start()
+
     for d in range(-YREACH, YREACH + 1):
         if d:
             met = met + nz * has(ay, d).astype(jnp.int32)
@@ -80,10 +84,6 @@
     for rel in range(1, nz):
         pl.semaphore_signal(barrier, inc=1, device_id={az: lax.rem(gz + rel, nz)}, device_id_type=MESH)
 
-    loads = [pltpu.make_async_copy(a, b, in_sem.at[i]) for i, (a, b) in enumerate(((phase, ph), (conc, co), (factors, factor), (pot, po), (src, so)))]
-    for load in loads:
-        load.start()
-
     for axis, bufs in ((ax, (xr1, xr2)), (ay, (yr1, yr3, yr4, yr6, yr7)), (az, (zr1, zr3, zr4, zr6, zr7))):
         for side, d in ((0, -1), (1, 1)):
 
@@ -91,14 +91,6 @@
             def _(bufs=bufs, side=side):
                 for buf in bufs:
                     buf[side] = jnp.zeros(buf.shape[1:], jnp.float32)
-
-    blocks = [(ax, d, qb, XREACH + d) for d in range(-XREACH, XREACH + 1) if d]
-    blocks += [(ay, d, gb, YREACH + d) for d in (-1, 1)] + [(ay, d, gh, i) for i, d in enumerate(HALVES)]
-    for axis, d, buf, slot in blocks:
-
-        @pl.when(jnp.logical_not(has(axis, d)))
-        def _(buf=buf, slot=slot):
-            buf[slot] = jnp.zeros(buf.shape[1:], jnp.float32)
 
     pending = []
     used = [0]
@@ -242,7 +234,6 @@
     zpack(zs1, [fine[x][a] for a in range(4) for x in range(8)], 1, 1)
     xs1[0] = fine[0]
     xs1[1] = fine[7]
-    loads[4].wait()
 
     pl.semaphore_wait(barrier, met)
 
@@ -263,6 +254,7 @@
         a, b = fine[2 * i + 1], fine[2 * i + 2]
         inner.append(flux(a[0], a[1:], b))
 
+    loads[4].wait()
     wait_y1()
     wait_z1()
     zlow, zhigh = zr1[0], zr1[1]
@@ -462,6 +454,14 @@
         start([(direct + XREACH - d, qb.at[XREACH], qb.at[XREACH - d], {ax: gx + d})], inside)
 
     drain(old)
+    blocks = [(ax, d, qb, XREACH + d) for d in range(-XREACH, XREACH + 1) if d]
+    blocks += [(ay, d, gb, YREACH + d) for d in (-1, 1)] + [(ay, d, gh, i) for i, d in enumerate(HALVES)]
+    for axis, d, buf, slot in blocks:
+
+        @pl.when(jnp.logical_not(has(axis, d)))
+        def _(buf=buf, slot=slot):
+            buf[slot] = jnp.zeros(buf.shape[1:], jnp.float32)
+
     packed = jnp.concatenate([merge4(*(e1[i][f] for i in four)) for f in range(FIELDS)], axis=0)
     r = lax.broadcasted_iota(jnp.int32, (WIDE, WIDE), 0)
     c = lax.broadcasted_iota(jnp.int32, (WIDE, WIDE), 1)

time: 66.6 us -> 66.6 us (level)
  no operation moved by 1% of the time
where the time goes in v6:
time: 66.6 us; the launch traced here: 66.5 us
  Pallas kernels  64 us (96%)
  local copies, waits for them, and re-layouts  1.82 us (3%)
    pallas_call x1, Pallas kernels, local(): pl.pallas_call(functools.partial(kernel, names, sizes), out_shape=(jax.Sh...  64 us
    unnamed x4, local copies, waits for them, and re-layouts  1.82 us

profile of v6, /device:TPU:69, one launch (start us, length us, event | category | flops | bytes accessed | tf_op | source)
XLA Modules:
  0.0 66.5 jit_solution(12795397455832176938)
XLA Ops:
  0.6 0.0 copy-start
  0.6 0.6 copy-done
  1.3 64.0 %shard_map.68 = (f32[3,4,4,128]{3,2,1,0:T(4,128)S(1)}, f32[3,1,1,128]{3,2,1,0:T(1,128)S(1)}) custom-call(s32[8,8,256]{2,1,0:T(8,128)} %phase.1, f32[8,8,256]{2,1,0:T(8,128)} %conc.1, f32[3,8,8,256]{3,2,1,0:T(8,128)} %pot.1, f32[3,8,8,256]{3,2,1,0:T(8,128)} %src.1, f32[3]{0:T(128)S(1)} %copy-done), custom_call_target="tpu_custom_call" | custom-call | tf_op jit(solution)/shard_map/pallas_call | solution.py:699
  65.3 0.6 copy.9
  65.9 0.6 copy.10
Async XLA Ops:
  0.6 0.7 copy-start

commit v7 on v5

--- a/solution.py
+++ b/solution.py
@@ -265,6 +265,7 @@
 
     wait_y1()
     wait_z1()
+    early.forward()
     zlow, zhigh = zr1[0], zr1[1]
     part, ypart, zpart = [], [], []
     for x in range(8):
@@ -330,7 +331,6 @@
         xs2[side, 1] = merge4(r1[edge][0], r1[edge][1], r1[edge][2], sx[face])
         xs2[side, 2] = merge4(ylo[edge], yhi[edge], zlo[edge], zhi[edge])
     late = Crossing(xs2, xr2, xk2, [pl.ds(0, 2), pl.ds(2, 1)], ([0, 1], [XROW - 1, XROW - 2]))
-    early.forward()
     late.forward()
     early.finish()
     for side, edge in ((0, 0), (1, XROW - 1)):

time: 66.6 us -> 67 us (level)
  no operation moved by 1% of the time
where the time goes in v7:
time: 67 us; the launch traced here: 66.7 us
  Pallas kernels  64.2 us (96%)
  local copies, waits for them, and re-layouts  1.82 us (3%)
    pallas_call x1, Pallas kernels, local(): pl.pallas_call(functools.partial(kernel, names, sizes), out_shape=(jax.Sh...  64.2 us
    unnamed x4, local copies, waits for them, and re-layouts  1.82 us

profile of v7, /device:TPU:69, one launch (start us, length us, event | category | flops | bytes accessed | tf_op | source)
XLA Modules:
  0.0 66.7 jit_solution(3135588040814240678)
XLA Ops:
  0.6 0.0 copy-start
  0.6 0.6 copy-done
  1.3 64.2 %shard_map.68 = (f32[3,4,4,128]{3,2,1,0:T(4,128)S(1)}, f32[3,1,1,128]{3,2,1,0:T(1,128)S(1)}) custom-call(s32[8,8,256]{2,1,0:T(8,128)} %phase.1, f32[8,8,256]{2,1,0:T(8,128)} %conc.1, f32[3,8,8,256]{3,2,1,0:T(8,128)} %pot.1, f32[3,8,8,256]{3,2,1,0:T(8,128)} %src.1, f32[3]{0:T(128)S(1)} %copy-done), custom_call_target="tpu_custom_call" | custom-call | tf_op jit(solution)/shard_map/pallas_call | solution.py:699
  65.5 0.6 copy.9
  66.1 0.6 copy.10
Async XLA Ops:
  0.6 0.7 copy-start
